TPU v7x, 128 devices: a whole 4x4x4 slice. The times are simulated.
128 devices in a mesh: member: 4 (over x), section: 2 (over core), dp: 16 (over z, y).
Axes of the slice: x: 4, y: 4, z: 4, core: 2. Of those that a mesh axis runs over, the one named last changes fastest.
Arguments:
- embeds: bfloat16 [4, 16, 2, 64, 4096], P('member', 'dp'), may hold values from -6 to 6
- lengths: int32 [16, 2], P('dp'), may hold values from 1 to 64, as said below
- route: int32 [16], P('dp'), may hold values from 0 to 15, each once
- w_query: bfloat16 [4, 2, 4096, 2048], P('member', 'section', 'dp'), may hold values from -0.09375 to 0.09375
- w_keyval: bfloat16 [4, 2, 4096, 1024], P('member', 'section', 'dp'), may hold values from -0.09375 to 0.09375
- w_out: bfloat16 [4, 2, 2048, 4096], P('member', 'section', 'dp'), may hold values from -0.125 to 0.125
- norm_gain: float32 [4, 2, 4096], P('member', 'section'), may hold values from 0.5 to 1.5
- head: float32 [4, 4096], P('member'), may hold values from -0.09375 to 0.09375
Outputs:
- scores: float32 [16, 2], P('dp')
- grad_out: float32 [4, 2, 2048, 4096], P('member', 'section', 'dp')
- grad_gain: float32 [4, 2, 4096], P('member', 'section', 'dp')
Inputs may be any that keep to these rules, and one draw needn't show every extreme that they name: `lengths`: some sequence fills all 64 positions. `route`: every balanced slot receives exactly one pair.
All inputs are finite; a program needn't handle non-finite values.
Results may differ from a plain program's by a relative error of at most 0.029.
Values may be sent and summed in bfloat16 or wider, within the bound.
A program may use at most 192 MiB of HBM per device.

v0:
```python
import jax
import jax.numpy as jnp
from jax import lax
from jax.sharding import PartitionSpec as P

HS = 128


EPS = 1e-05


def from_behind(value, axis, steps):
    count = lax.axis_size(axis)
    first, last = (max(0, -steps), min(count, count - steps))
    return lax.ppermute(value, axis, [(source, source + steps) for source in range(first, last)])


def unit_rows(widened):
    return widened * lax.rsqrt(jnp.mean(widened * widened, -1, keepdims=True) + EPS)


def rms_scale(widened, norm_scale):
    return unit_rows(widened) * norm_scale


def attend(queries, keyvals):
    seq_count, positions, feat_width = queries.shape
    head_count = feat_width // HS
    shared_heads = keyvals.shape[-1] // (2 * HS)
    group_size = head_count // shared_heads
    query_heads = queries.reshape(seq_count, positions, shared_heads, group_size, HS)
    key_rows = keyvals[..., : shared_heads * HS].reshape(seq_count, positions, shared_heads, HS)
    value_rows = keyvals[..., shared_heads * HS :].reshape(seq_count, positions, shared_heads, HS)
    logits = jnp.einsum(
        "nqhgd,nkhd->nhgqk", query_heads, key_rows, precision=lax.Precision.HIGHEST
    ) * HS ** (-0.5)
    causal = jnp.arange(positions)[:, None] >= jnp.arange(positions)[None, :]
    weights = jnp.where(causal, jnp.exp(jnp.where(causal, logits, 0.0)), 0.0)
    weights = weights / jnp.sum(weights, -1, keepdims=True)
    weights = lax.optimization_barrier(weights.astype(jnp.bfloat16)).astype(jnp.float32)
    context = jnp.einsum("nhgqk,nkhd->nqhgd", weights, value_rows, precision=lax.Precision.HIGHEST)
    return context.reshape(seq_count, positions, feat_width)


def segment_forward(hidden, norm_scale, query_proj, keyval_proj, out_proj):
    seq_count, positions, model_width = hidden.shape
    widened = hidden.astype(jnp.float32)
    normed = (
        rms_scale(widened, norm_scale)
        .astype(jnp.bfloat16)
        .reshape(seq_count * positions, model_width)
    )
    queries = jnp.dot(normed, query_proj, preferred_element_type=jnp.float32).astype(jnp.bfloat16)
    keyvals = jnp.dot(normed, keyval_proj, preferred_element_type=jnp.float32).astype(jnp.bfloat16)
    context = attend(
        queries.reshape(seq_count, positions, -1).astype(jnp.float32),
        keyvals.reshape(seq_count, positions, -1).astype(jnp.float32),
    )
    context = context.astype(jnp.bfloat16).reshape(seq_count * positions, -1)
    update = jnp.dot(context, out_proj, preferred_element_type=jnp.float32)
    output = (widened + update.reshape(seq_count, positions, model_width)).astype(jnp.bfloat16)
    return (output, (hidden, queries, keyvals, context))


def branch_back(grad_now, residuals, norm_scale, query_proj, keyval_proj, out_proj):
    hidden, queries, keyvals, context = residuals
    seq_count, positions, model_width = hidden.shape
    row_count = seq_count * positions
    grad_rows = grad_now.reshape(row_count, model_width)
    grad_context = lax.dot_general(
        grad_rows, out_proj, (((1,), (1,)), ((), ())), preferred_element_type=jnp.float32
    )
    _, pull_attend = jax.vjp(
        attend,
        queries.reshape(seq_count, positions, -1).astype(jnp.float32),
        keyvals.reshape(seq_count, positions, -1).astype(jnp.float32),
    )
    grad_query, grad_keyval = pull_attend(grad_context.reshape(seq_count, positions, -1))
    grad_normed = lax.dot_general(
        grad_query.astype(jnp.bfloat16).reshape(row_count, -1),
        query_proj,
        (((1,), (1,)), ((), ())),
        preferred_element_type=jnp.float32,
    )
    grad_normed = grad_normed + lax.dot_general(
        grad_keyval.astype(jnp.bfloat16).reshape(row_count, -1),
        keyval_proj,
        (((1,), (1,)), ((), ())),
        preferred_element_type=jnp.float32,
    )
    widened = hidden.astype(jnp.float32)
    _, pull_norm = jax.vjp(lambda rows_in: rms_scale(rows_in, norm_scale), widened)
    (grad_hidden,) = pull_norm(grad_normed.reshape(seq_count, positions, model_width))
    new_grad = (grad_now.astype(jnp.float32) + grad_hidden).astype(jnp.bfloat16)
    return (new_grad, grad_normed)


def pick_last(final, seq_lens):
    last_mask = jnp.arange(final.shape[1])[None, :] == (seq_lens - 1)[:, None]
    picked = jnp.sum(jnp.where(last_mask[:, :, None], final.astype(jnp.float32), 0.0), axis=1)
    return (picked, last_mask)


def score_of(last_rows, head_vec):
    return jnp.sum(rms_scale(last_rows, head_vec), -1)


def seed_of(final, seq_lens, head_vec, ensemble):
    last_rows, last_mask = pick_last(final, seq_lens)
    spread = jax.nn.sigmoid(ensemble[:, 1] - ensemble[:, 0])
    direction = jnp.stack([-spread, spread], -1).reshape(-1)
    _, pull_score = jax.vjp(lambda rows_in: score_of(rows_in, head_vec), last_rows)
    (grad_last,) = pull_score(direction)
    return jnp.where(last_mask[:, :, None], grad_last[:, None, :], 0.0).astype(jnp.bfloat16)


def body(embeds, lengths, route, w_query, w_keyval, w_out, norm_gain, head):
    segments = lax.axis_size("section")
    segment_index = lax.axis_index("section")
    group_index = lax.axis_index("dp")
    pair_dev = embeds.shape[1]
    positions = embeds.shape[3]
    model_width = embeds.shape[4]
    seq_count = 2 * pair_dev
    row_count = seq_count * positions
    lens_all, route_all = (
        lax.all_gather(lengths, "dp", axis=0, tiled=True),
        lax.all_gather(route, "dp", axis=0, tiled=True),
    )
    my_slots = group_index * pair_dev + jnp.arange(pair_dev, dtype=jnp.int32)
    owner_mask = route_all[None, :] == my_slots[:, None]
    flat_pairs = embeds.reshape(pair_dev, 2 * positions * model_width)
    selector = (route_all[None, :] == my_slots[:, None]).astype(jnp.bfloat16)
    placed = jnp.dot(
        selector,
        lax.all_gather(flat_pairs, "dp", axis=0, tiled=True),
        preferred_element_type=jnp.float32,
    )
    hidden = placed.astype(jnp.bfloat16).reshape(seq_count, positions, model_width)
    seq_lens = jnp.sum(jnp.where(owner_mask[:, :, None], lens_all[None, :, :], 0), axis=1).reshape(
        seq_count
    )
    query_full, keyval_full, out_full = (
        lax.all_gather(w_query[0, 0], "dp", axis=0, tiled=True),
        lax.all_gather(w_keyval[0, 0], "dp", axis=0, tiled=True),
        lax.all_gather(w_out[0, 0], "dp", axis=0, tiled=True),
    )
    norm_scale = norm_gain[0, 0]
    head_vec = head[0]
    blank = (
        jnp.zeros_like(hidden),
        jnp.zeros((row_count, query_full.shape[1]), jnp.bfloat16),
        jnp.zeros((row_count, keyval_full.shape[1]), jnp.bfloat16),
        jnp.zeros((row_count, out_full.shape[0]), jnp.bfloat16),
    )

    def active_forward(segment_input):
        return segment_forward(segment_input, norm_scale, query_full, keyval_full, out_full)

    def resting_forward(segment_input):
        return (jnp.zeros_like(segment_input), blank)

    residuals = blank
    output = hidden
    for segment_turn in range(segments):
        is_mine = segment_index == segment_turn
        output, stored = lax.cond(is_mine, active_forward, resting_forward, hidden)
        residuals = jax.tree.map(
            lambda earlier, latest: jnp.where(is_mine, latest, earlier), residuals, stored
        )
        if segment_turn + 1 < segments:
            hidden = from_behind(output, "section", 1)
    last_rows, _ = pick_last(output, seq_lens)
    own_scores = jnp.where(
        segment_index == segments - 1, score_of(last_rows, head_vec), 0.0
    ).reshape(pair_dev, 2)
    totals = lax.psum(own_scores, ("member", "section"))
    ensemble = totals / lax.axis_size("member")
    grad_now = seed_of(output, seq_lens, head_vec, ensemble)
    kept_grad = jnp.zeros_like(grad_now)
    gain_accum = jnp.zeros((model_width,), jnp.float32)

    def active_back(grad_in):
        new_grad, grad_normed = branch_back(
            grad_in, residuals, norm_scale, query_full, keyval_full, out_full
        )
        unit_part = unit_rows(residuals[0].astype(jnp.float32)).reshape(row_count, model_width)
        return (new_grad, jnp.sum(grad_normed * unit_part, 0))

    def resting_back(grad_in):
        return (jnp.zeros_like(grad_in), jnp.zeros((model_width,), jnp.float32))

    for segment_turn in reversed(range(segments)):
        is_mine = segment_index == segment_turn
        new_grad, gain_part = lax.cond(is_mine, active_back, resting_back, grad_now)
        kept_grad = jnp.where(is_mine, grad_now, kept_grad)
        gain_accum = gain_accum + gain_part
        if segment_turn > 0:
            grad_now = from_behind(new_grad, "section", -1)
    grad_rows = kept_grad.reshape(row_count, model_width)
    context_rows = residuals[3]
    out_term = lax.dot_general(
        context_rows, grad_rows, (((0,), (0,)), ((), ())), preferred_element_type=jnp.float32
    )
    out_part, gain_total = (
        lax.psum_scatter(
            out_term.astype(jnp.bfloat16), "dp", scatter_dimension=0, tiled=True
        ).astype(jnp.float32),
        lax.psum_scatter(
            gain_accum.astype(jnp.bfloat16), "dp", scatter_dimension=0, tiled=True
        ).astype(jnp.float32),
    )
    return (ensemble, out_part.reshape(1, 1, -1, model_width), gain_total.reshape(1, 1, -1))


def solution(mesh):
    placed = (
        P("member", "dp", None, None, None),
        P("dp", None),
        P("dp"),
        P("member", "section", "dp", None),
        P("member", "section", "dp", None),
        P("member", "section", "dp", None),
        P("member", "section", None),
        P("member", None),
    )
    return jax.shard_map(
        body,
        mesh=mesh,
        in_specs=placed,
        out_specs=(P("dp", None), P("member", "section", "dp", None), P("member", "section", "dp")),
        check_vma=False,
    )
```

profile of v0, /device:TPU:1, one launch (start us, length us, event | category | flops | bytes accessed | tf_op | source)
XLA Modules:
  0.0 774.1 jit_solution(141378270086296001)
XLA Ops:
  7.2 4.1 reshape.381
  11.4 0.7 all-gather.10.cloned.1.call-update
  14.8 0.8 dynamic-update-slice
  15.5 14.8 %all-reduce.4 = s32[16]{0:T(128)S(1)} all-reduce(s32[16]{0:T(128)S(1)} %dynamic-update-slice), channel_id=1, replica_groups=mesh['member'=4,'section'=2,'dp'=16] {'dp'}, use_global_device_ids=true, to_apply=%add.4 | all-reduce | flops 16 | bytes 128
  30.3 181.6 %all-gather.16.cloned.1.call-done = bf16[16,1,524288]{2,1,0:T(2,128)(2,1)} async-done(((bf16[1,1,524288]{2,1,0:T(2,128)(2,1)}), bf16[16,1,524288]{2,1,0:T(2,128)(2,1)}) %all-gather.16.cloned.1.call-update) | async-done | bytes 16777232 | tf_op jit(solution)/shard_map/all_gather | solution.py:136
  211.9 32.2 %fusion.89 = f32[1,524288]{1,0:T(1,128)S(1)} fusion(bf16[16,1,524288]{2,1,0:T(2,128)(2,1)} %all-gather.16.cloned.1.call-done, pred[16]{0:T(512)(128)(4,1)S(1)} %broadcast_compare_fusion), kind=kOutput, calls=%fused_computation.136 | convolution fusion | flops 16777216 | bytes 18874384 | tf_op jit(solution)/shard_map/dot_general | solution.py:134
  244.3 40.3 %all-gather.10.cloned.1.call-done = bf16[1,1,4096,1024]{3,2,1,0:T(8,128)(2,1)} async-done(((bf16[1,1,256,1024]{3,2,1,0:T(8,128)(2,1)}), bf16[1,1,4096,1024]{3,2,1,0:T(8,128)(2,1)}) %all-gather.10.cloned.1.call-update) | async-done | bytes 8388624 | tf_op jit(solution)/shard_map/all_gather | solution.py:145
  284.6 113.2 %all-gather.12.cloned.1.call-done = bf16[1,1,4096,2048]{3,2,1,0:T(8,128)(2,1)} async-done(((bf16[1,1,256,2048]{3,2,1,0:T(8,128)(2,1)}), bf16[1,1,4096,2048]{3,2,1,0:T(8,128)(2,1)}) %all-gather.12.cloned.1.call-update) | async-done | bytes 16777232 | tf_op jit(solution)/shard_map/all_gather | solution.py:144
  397.8 113.1 %all-gather.14.cloned.1.call-done = bf16[1,1,2048,4096]{3,2,1,0:T(8,128)(2,1)} async-done(((bf16[1,1,128,4096]{3,2,1,0:T(8,128)(2,1)}), bf16[1,1,2048,4096]{3,2,1,0:T(8,128)(2,1)}) %all-gather.14.cloned.1.call-update) | async-done | bytes 16777232 | tf_op jit(solution)/shard_map/all_gather | solution.py:146
  510.9 4.6 conditional.4
  510.9 1.1 broadcast.250
  511.9 1.1 broadcast.250.clone
  513.0 0.9 broadcast.251
  513.9 0.8 broadcast.251.clone
  514.7 0.7 broadcast_in_dim.131
  515.4 1.3 collective-permute-start
  516.7 15.7 %all-gather.3 = s32[16,1,2]{2,1,0:T(1,128)S(1)} all-gather(s32[1,1,2]{2,1,0:T(1,128)S(1)} %bitcast.245), channel_id=1, replica_groups=mesh['member'=4,'section'=2,'dp'=16] {'dp'}, dimensions={0}, use_global_device_ids=true | all-gather | bytes 136 | tf_op jit(solution)/shard_map/all_gather | solution.py:127
  532.7 13.5 %collective-permute-done = bf16[2,64,4096]{2,1,0:T(8,128)(2,1)S(1)} collective-permute-done((bf16[2,64,4096]{2,1,0:T(8,128)(2,1)}, bf16[2,64,4096]{2,1,0:T(8,128)(2,1)S(1)}, u32[]{:S(2)}, u32[]{:S(2)}) %collective-permute-start) | collective-permute-done | bytes 1048608 | tf_op jit(solution)/shard_map/ppermute | solution.py:15
  546.2 27.0 %conditional.5 = (bf16[2,64,4096]{2,1,0:T(8,128)(2,1)}, bf16[128,2048]{1,0:T(8,128)(2,1)S(1)}, bf16[128,1024]{1,0:T(8,128)(2,1)}, bf16[128,2048]{1,0:T(8,128)(2,1)S(1)}, f32[2,64,4096]{2,1,0:T(8,128)}) conditional(s32[]{:T(128)} %convert_element_type.180, () %tuple.45, (bf16[2,64,4096]{2,1,0:T(8,128)(2,1)S(1)}, f32[1,1,4096]{2,1,0:T(1,128)S(1)}, ...), branch_computations={%region_5.6_spmd, %region_6.9_spmd} | conditional | flops 5442902016 | bytes 67136632 | solution.py:167
  546.9 4.6 convolution_convert_fusion.5
  551.7 8.1 %convolution_convert_fusion.3 = bf16[128,2048]{1,0:T(8,128)(2,1)S(1)} fusion(bf16[128,4096]{1,0:T(8,128)(2,1)S(1)} %fusion.30, bf16[4096,2048]{1,0:T(8,128)(2,1)} %get-tuple-element.62), kind=kOutput, calls=%fused_computation.28 | convolution fusion | flops 2147745792 | bytes 18350080 | tf_op jit(solution)/shard_map/cond/branch_1_fun/dot_general | solution.py:53
  562.2 9.4 %fusion.26 = f32[2,64,4096]{2,1,0:T(8,128)} fusion(bf16[2,64,2048]{2,1,0:T(8,128)(2,1)S(1)} %convert_element_type.153, bf16[2048,4096]{1,0:T(8,128)(2,1)} %get-tuple-element.64, bf16[2,64,4096]{2,1,0:T(8,128)(2,1)S(1)} %get-tuple-element.154), kind=kOutput, calls=%fused_computation.27 | convolution fusion | flops 2149580800 | bytes 20447232 | tf_op jit(solution)/shard_map/cond/branch_1_fun/dot_general | solution.py:60
  572.1 1.0 copy.209
  573.3 2.1 select_reduce_fusion.2
  575.8 11.6 %psum.7 = f32[1,2]{1,0:T(1,128)S(1)} all-reduce(f32[1,2]{1,0:T(1,128)S(1)} %fusion.100), channel_id=1, replica_groups=mesh['member'=4,'section'=2,'dp'=16] {'member','section'}, use_global_device_ids=true, to_apply=%region_12.13 | all-reduce | flops 2 | bytes 16 | tf_op jit(solution)/shard_map/psum | solution.py:177
  589.9 1.8 select_convert_fusion
  591.8 47.2 %conditional.6 = (bf16[2,64,4096]{2,1,0:T(8,128)(2,1)S(1)}, f32[4096]{0:T(1024)S(1)}) conditional(s32[]{:T(128)} %convert_element_type.180, () %tuple.49, (bf16[2,64,4096]{2,1,0:T(8,128)(2,1)S(1)}, bf16[2048,4096]{1,0:T(8,128)(2,1)}, bf16[128,1024]{1,0:T(8,128)(2,1)S(1)}, bf16[128,2048]{1,0:T(8,128)(2,1)S(1)}, bf16[4096,2048]{1,0:T(8,128)(2,1)}, ...), branch_computations={%region_14.15_spmd, %region_15.21_spmd} | conditional | flops 6221466624 | bytes 92397832 | solution.py:195
  593.5 2.5 select_reduce_fusion
  596.6 9.2 %convolution_bitcast_fusion = f32[2,4,128,4,64]{2,4,3,1,0:T(8,128)S(1)} fusion(bf16[4,4,128,4096,1]{3,2,1,0,4:T(8,128)(2,1)} %bitcast.210, bf16[2,64,4096]{2,1,0:T(8,128)(2,1)S(1)} %get-tuple-element.65), kind=kOutput, calls=%fused_computation.64 | convolution fusion | flops 2147483648 | bytes 18874368 | tf_op jit(solution)/shard_map/cond/branch_1_fun/dot_general | solution.py:70
  606.5 1.6 convolution_convert_fusion.7
  608.2 1.8 divide_convert_fusion.2
  610.1 1.7 convolution_bitcast_fusion.1
  611.7 0.8 convolution_bitcast_fusion.2
  612.6 0.7 add_convert_fusion
  613.3 1.5 fusion.48
  615.6 12.7 %fusion.109 = f32[128,4096]{1,0:T(8,128)} fusion(bf16[128,2048]{1,0:T(8,128)(2,1)S(1)} %convert_element_type.161, bf16[4096,2048]{1,0:T(8,128)(2,1)} %get-tuple-element.69), kind=kOutput, calls=%fused_computation.180 | convolution fusion | flops 2147483648 | bytes 19398656 | tf_op jit(solution)/shard_map/cond/branch_1_fun/dot_general | solution.py:79
  628.4 6.9 convolution_add_fusion
  635.8 1.7 convert_multiply_fusion.1
  637.8 0.9 copy-done.12
  639.6 1.3 collective-permute-start.1
  640.9 2.2 collective-permute-done.1
  643.1 1.1 select_select_fusion
  644.3 9.3 %convolution_convert_fusion.10 = bf16[2048,4096]{1,0:T(8,128)(2,1)} fusion(bf16[128,4096]{1,0:T(8,128)(2,1)S(1)} %bitcast.219, bf16[128,2048]{1,0:T(8,128)(2,1)} %copy-done.4, bf16[128,2048]{1,0:T(8,128)(2,1)} %get-tuple-element.98, pred[]{:T(512)S(6)} %eq.25, pred[]{:T(512)S(6)} %eq.19), kind=kOutput, calls=%fused_computation.139 | convolution fusion | flops 2156396544 | bytes 18874370 | tf_op jit(solution)/shard_map/dot_general | solution.py:202
  654.6 1.3 conditional.7
  655.9 0.7 add_convert_fusion.2
  656.6 33.2 %all-reduce.5 = bf16[4096]{0:T(1024)(128)(2,1)S(1)} all-reduce(bf16[4096]{0:T(1024)(128)(2,1)S(1)} %add_convert_fusion.2), channel_id=6, replica_groups=mesh['member'=4,'section'=2,'dp'=16] {'dp'}, use_global_device_ids=true, to_apply=%region_28.29.clone | all-reduce | flops 4096 | bytes 16384
  690.5 73.8 %reduce-scatter.2.cloned.1.call-done = bf16[128,4096]{1,0:T(8,128)(2,1)} async-done(((bf16[2048,4096]{1,0:T(8,128)(2,1)}), bf16[128,4096]{1,0:T(8,128)(2,1)}) %reduce-scatter.2.cloned.1.call-update) | async-done | bytes 1048592 | tf_op jit(solution)/shard_map/reduce_scatter | solution.py:206
  764.3 2.8 bitcast_convert_fusion
  (108 shorter events, 13.8 us)
Async XLA Ops:
  7.2 204.7 %all-gather.16.cloned.1.call-start = ((), (), s32[]{:S(2)}) async-start(), calls=%async_computation.5 | async-start | bytes 35651584 | tf_op jit(solution)/shard_map/all_gather | solution.py:136
  11.3 2.8 copy-start.30
  11.3 273.2 %all-gather.10.cloned.1.call-start = ((), (), s32[]{:S(2)}) async-start(), calls=%async_computation.2 | async-start | bytes 8912896 | tf_op jit(solution)/shard_map/all_gather | solution.py:145
  12.1 385.7 %all-gather.12.cloned.1.call-start = ((), (), s32[]{:S(2)}) async-start(), calls=%async_computation.3 | async-start | bytes 17825792 | tf_op jit(solution)/shard_map/all_gather | solution.py:144
  12.8 498.0 %all-gather.14.cloned.1.call-start = ((), (), s32[]{:S(2)}) async-start(), calls=%async_computation.4 | async-start | bytes 17825792 | tf_op jit(solution)/shard_map/all_gather | solution.py:146
  13.4 750.9 %reduce-scatter.2.cloned.1.call-start = ((), (), s32[]{:S(2)}) async-start(), calls=%async_computation.1 | async-start | bytes 17825792 | tf_op jit(solution)/shard_map/reduce_scatter | solution.py:206
  244.1 266.7 %copy-start.13 = (f32[1,1,4096]{2,1,0:T(1,128)S(1)}, f32[1,1,4096]{2,1,0:T(1,128)}, u32[]{:S(2)}) copy-start(f32[1,1,4096]{2,1,0:T(1,128)} %param.22) | copy-start | bytes 49156
  510.8 5.9 copy-start.32
  515.4 30.8 %collective-permute-start = (bf16[2,64,4096]{2,1,0:T(8,128)(2,1)}, bf16[2,64,4096]{2,1,0:T(8,128)(2,1)S(1)}, u32[]{:S(2)}, u32[]{:S(2)}) collective-permute-start(bf16[2,64,4096]{2,1,0:T(8,128)(2,1)} %get-tuple-element.95), channel_id=1, source_target_pairs={{0,16},{1,17},{2,18},{3,19},{4,20},{5,21},{6,22},{7,23},{8,24},{9,... | collective-permute-start | bytes 3145736 | tf_op jit(solution)/shard_map/ppermute | solution.py:15
  532.7 57.2 %copy-start.29 = (pred[2,64]{1,0:T(4,128)(4,1)}, pred[2,64]{1,0:T(4,128)(4,1)S(1)}, u32[]{:S(2)}) copy-start(pred[2,64]{1,0:T(4,128)(4,1)S(1)} %iota_compare_fusion.4) | copy-start | bytes 388
  551.6 8.2 %copy-start.7 = (bf16[128,1024]{1,0:T(8,128)(2,1)}, bf16[128,1024]{1,0:T(8,128)(2,1)S(1)}, u32[]{:S(2)}) copy-start(bf16[128,1024]{1,0:T(8,128)(2,1)S(1)} %convolution_convert_fusion.5) | copy-start | bytes 786436 | tf_op jit(solution)/shard_map/cond
  559.8 1.2 copy-start.2
  571.7 1.4 copy-start.3
  573.3 16.5 %copy-start.4 = (bf16[128,2048]{1,0:T(8,128)(2,1)}, bf16[128,2048]{1,0:T(8,128)(2,1)S(1)}, u32[]{:S(2)}) copy-start(bf16[128,2048]{1,0:T(8,128)(2,1)S(1)} %get-tuple-element.97) | copy-start | bytes 1572868
  573.3 2.3 copy-start.19
  573.3 16.6 %copy-start.6 = (bf16[128,1024]{1,0:T(8,128)(2,1)S(1)}, bf16[128,1024]{1,0:T(8,128)(2,1)}, u32[]{:S(2)}) copy-start(bf16[128,1024]{1,0:T(8,128)(2,1)} %get-tuple-element.100) | copy-start | bytes 786436
  573.3 16.6 %copy-start.8 = (bf16[128,1024]{1,0:T(8,128)(2,1)S(1)}, bf16[128,1024]{1,0:T(8,128)(2,1)}, u32[]{:S(2)}) copy-start(bf16[128,1024]{1,0:T(8,128)(2,1)} %get-tuple-element.99) | copy-start | bytes 786436
  587.4 1.9 copy-start.31
  589.8 2.0 copy-start.18
  589.9 1.9 copy-start
  593.5 3.1 copy-start.14
  596.0 0.6 copy-start.23
  606.5 1.6 copy-start.10
  606.5 3.5 copy-start.15
  606.5 3.5 copy-start.24
  606.5 3.5 copy-start.26
  611.7 1.6 copy-start.20
  615.6 12.7 %copy-start.9 = (bf16[2,64,1024]{2,1,0:T(8,128)(2,1)S(1)}, bf16[2,64,1024]{2,1,0:T(8,128)(2,1)}, u32[]{:S(2)}) copy-start(bf16[2,64,1024]{2,1,0:T(8,128)(2,1)} %add_convert_fusion) | copy-start | bytes 786436 | tf_op jit(solution)/shard_map/cond
  637.5 1.2 copy-start.12
  639.0 0.6 copy-start.25
  639.6 3.6 collective-permute-start.1
  653.5 1.0 copy-start.1
Sparse Core Ops, SparseCore 0:
  11.5 200.4 all-gather.15
  214.0 70.4 all-gather.9
  286.7 110.9 all-gather.11
  399.8 111.0 all-gather.13
  653.7 110.5 reduce-scatter.1
where the time goes:
time: 786 us; the launch traced here: 774 us
  waiting for transfers between devices  540 us (69%)
  matrix products  102 us (13%)
  blocking collectives  75.4 us (10%)
  local copies, waits for them, and re-layouts  18.1 us (2%)
  other arithmetic  17.5 us (2%)
  between operations  17.3 us (2%)
    all_gather x1, waiting for transfers between devices, body(): lax.all_gather(flat_pairs, 'dp', axis=0, tiled=True)  182 us
    all_gather x1, waiting for transfers between devices, body(): lax.all_gather(w_query[0, 0], 'dp', axis=0, tiled=True)  113 us
    all_gather x1, waiting for transfers between devices, body(): lax.all_gather(w_out[0, 0], 'dp', axis=0, tiled=True)  113 us
    reduce_scatter x1, waiting for transfers between devices, body(): lax.psum_scatter(out_term.astype(jnp.bfloat16), 'dp', scatter_dimension=0...  73.8 us
    unnamed x2, blocking collectives  48 us
    all_gather x1, waiting for transfers between devices, body(): lax.all_gather(w_keyval[0, 0], 'dp', axis=0, tiled=True)  40.3 us
    dot_general x1, matrix products, body(): jnp.dot(selector, lax.all_gather(flat_pairs, 'dp', axis=0, tiled=True), p...  32.2 us
  transfers between devices with their start and end apart: 7, of which 7 were waited for; matrix products, arithmetic and copies ran while one was open for 5% of the time, Pallas kernels for 0%

commit v1 on v0

v1 whole, which is shorter than its diff:
```python
import jax
import jax.numpy as jnp
from jax import lax
from jax.experimental import pallas as pl
from jax.experimental.pallas import tpu as pltpu
from jax.sharding import PartitionSpec as P

MESH = pl.DeviceIdType.MESH
F32 = jnp.float32
BF16 = jnp.bfloat16
EPS = 1e-05
HS = 128
SEQ = 64
D = 4096
RING = 4
N_DP = RING * RING
HEADS = 16
GROUP = HEADS // RING
QW = GROUP * HS
ROWS = RING * SEQ
BLK = D // N_DP
HALF = D // 2
SCALE = HS ** (-0.5)
N_SEMS = 112


def mm(a, b):
    return jnp.dot(a, b, preferred_element_type=F32)


def nt(a, b):
    return lax.dot_general(a, b, (((1,), (1,)), ((), ())), preferred_element_type=F32)


def tn(a, b):
    return lax.dot_general(a, b, (((0,), (0,)), ((), ())), preferred_element_type=F32)


def kernel(
    emb, lens, route, wq, wkv, wo, gain, head,
    scores_out, grad_out, gain_out,
    X, GA, HD, N, WQ, WKV, WO, WQ1, WO1, WKV1,
    QA, KVA, QB, KVB, WA, CTX, CTT, CTP, OP, FWD, LAND,
    H1, N1, KVA1, KC, VC, Q16,
    NL, HL, S1, R1, X1, T2, R2, S3, R3, X3, T4, R4, SCB, S6, R6, X6, T7, R7, DC,
    S8, R8, X8, T9, R9, GNL, XC, GC, GN, DKV,
    G, GP, DCT, DQB, DKVB, GOP, FWD2, LAND2, SG, RG, SP, PG,
    ssem, rsem, lsem,
):
    s = lax.axis_index("section")
    m = lax.axis_index("member")
    dp = lax.axis_index("dp")
    z = dp // RING
    y = dp % RING
    other = 1 - s
    zr, zl, zo = (z + 1) % RING, (z + 3) % RING, (z + 2) % RING
    yr, yl, yo = (y + 1) % RING, (y + 3) % RING, (y + 2) % RING
    at_zr, at_zl, at_zo = zr * RING + y, zl * RING + y, zo * RING + y
    at_yr, at_yl = z * RING + yr, z * RING + yl
    is0 = s == 0
    is1 = s == 1
    ids = {}
    pending = []

    def desc(name, src, dst, **dev):
        i = ids.setdefault(name, len(ids))
        return pltpu.make_async_remote_copy(
            src_ref=src, dst_ref=dst, send_sem=ssem.at[i], recv_sem=rsem.at[i],
            device_id=dev, device_id_type=MESH,
        )

    def guarded(cond, act):
        if cond is None:
            act()
        else:
            pl.when(cond)(act)

    def send(cond, *items):
        copies = [desc(name, src, dst, **dev) for name, src, dst, dev in items]

        def act():
            for c in copies:
                c.start()

        guarded(cond, act)

        def fin():
            for c in copies:
                c.wait_send()

        pending.append((cond, fin))

    def recv(cond, *items):
        copies = [desc(name, dst, dst, section=other) for name, dst in items]

        def act():
            for c in copies:
                c.wait_recv()

        guarded(cond, act)

    def exchange(name, src_of, land):
        i = ids.setdefault(name, len(ids))

        @pl.loop(1, N_DP)
        def _(k):
            peer = (dp + k) % N_DP
            pltpu.make_async_remote_copy(
                src_ref=src_of(peer, N_DP - 1 - k), dst_ref=land.at[k - 1],
                send_sem=ssem.at[i], recv_sem=rsem.at[i],
                device_id={"dp": peer}, device_id_type=MESH,
            ).start()

        whole = desc(name, land.at[pl.ds(0, N_DP - 1)], land.at[pl.ds(0, N_DP - 1)], section=other)
        pending.append((None, whole.wait_send))

    def landed(name, land):
        desc(name, land.at[pl.ds(0, N_DP - 1)], land.at[pl.ds(0, N_DP - 1)], section=other).wait_recv()

    def slot_of(h):
        return (dp + N_DP - 1 - h) % N_DP

    lx = pltpu.make_async_copy(emb.at[0, 0, s], X, lsem.at[0])
    lg = pltpu.make_async_copy(gain.at[0], GA.at[s], lsem.at[1])
    lh = pltpu.make_async_copy(head, HD, lsem.at[2])
    lx.start()
    lg.start()
    lh.start()
    wq_mine, wkv_mine, wo_mine = wq.at[0, 0], wkv.at[0, 0], wo.at[0, 0]

    def cols(ref, first, size):
        return ref.at[:, pl.ds(pl.multiple_of(first, HS), size)]

    def slices(dest_z):
        return (
            (cols(wq_mine, dest_z * QW, QW), WQ.at[y, z]),
            (cols(wkv_mine, dest_z * HS, HS), WKV.at[y, z, :, pl.ds(0, HS)]),
            (cols(wkv_mine, RING * HS + dest_z * HS, HS), WKV.at[y, z, :, pl.ds(HS, HS)]),
        )

    wo_rows = lambda yy: WO.at[pl.ds(pl.multiple_of(yy * HS, HS), HS)]
    local0 = [pltpu.make_async_copy(a, b, lsem.at[3 + n]) for n, (a, b) in enumerate(slices(z))]
    local0.append(pltpu.make_async_copy(wo_mine, wo_rows(y), lsem.at[6]))
    local1 = [
        pltpu.make_async_copy(wq_mine, WQ1, lsem.at[3]),
        pltpu.make_async_copy(wkv_mine, WKV1.at[y, z], lsem.at[4]),
        pltpu.make_async_copy(wo_mine, WO1, lsem.at[5]),
    ]

    @pl.when(is0)
    def _():
        for c in local0:
            c.start()

    @pl.when(is1)
    def _():
        for c in local1:
            c.start()

    barrier = pltpu.get_barrier_semaphore()

    @pl.loop(1, N_DP)
    def _(k):
        pl.semaphore_signal(barrier, inc=1, device_id={"dp": (dp + k) % N_DP}, device_id_type=MESH)

    for dm in range(4):
        for ds in range(2):
            if dm or ds:
                pl.semaphore_signal(
                    barrier, inc=1, device_id={"member": (m + dm) % 4, "section": (s + ds) % 2},
                    device_id_type=MESH,
                )
    for at in (at_yr, at_yl):
        pl.semaphore_signal(barrier, inc=1, device_id={"section": other, "dp": at}, device_id_type=MESH)
    pl.semaphore_wait(barrier, N_DP - 1 + 7 + 2)

    for far, at in ((1, at_zr), (3, at_zl), (2, at_zo)):
        dest = (z + far) % RING
        send(is0, *[(f"a2a{far}{n}", a, b, {"dp": at}) for n, (a, b) in enumerate(slices(dest))])
    mine = wo_rows(y)
    send(is0,
         ("wo_r", wo_mine, mine, {"dp": at_yr}),
         ("wo_l", wo_mine, mine, {"dp": at_yl}),
         ("wo_c", wo_mine, mine, {"section": 1}))
    send(None, ("gain", gain.at[0], GA.at[s], {"section": other}))

    lx.wait()
    lg.wait()
    lh.wait()
    recv(None, ("gain", GA.at[other]))
    my_rows = lambda zz: pl.ds(pl.multiple_of(zz * SEQ, SEQ), SEQ)

    @pl.loop(0, 4)
    def _(g):
        part = pl.ds(pl.multiple_of(g * 16, 16), 16)
        rows = X[part, :].astype(F32)
        unit = rows * lax.rsqrt(jnp.mean(rows * rows, -1, keepdims=True) + EPS)
        N[pl.ds(pl.multiple_of(z * SEQ + g * 16, 16), 16), :] = (unit * GA[0]).astype(BF16)

    def half_rows(ref, zz, half):
        return ref.at[pl.ds(pl.multiple_of(zz * SEQ + half * 32, 32), 32)]

    def ring_z1(name, ref):
        block = ref.at[my_rows(z)]
        send(None, (name + "r", block, block, {"dp": at_zr}), (name + "l", block, block, {"dp": at_zl}))

    def ring_z2(name, ref):
        recv(None, (name + "r", ref.at[my_rows(zl)]))
        a = half_rows(ref, zl, 0)
        send(None, (name + "R", a, a, {"dp": at_zr}))
        recv(None, (name + "l", ref.at[my_rows(zr)]))
        b = half_rows(ref, zr, 1)
        send(None, (name + "L", b, b, {"dp": at_zl}))

    def ring_z3(name, ref):
        recv(None, (name + "R", half_rows(ref, zo, 0)), (name + "L", half_rows(ref, zo, 1)))

    ring_z1("n", N)

    @pl.when(is0)
    def _():
        for c in local0:
            c.wait()

    for far, zz in ((1, zl), (3, zr), (2, zo)):
        recv(is0, (f"a2a{far}0", WQ.at[y, zz]),
             (f"a2a{far}1", WKV.at[y, zz, :, pl.ds(0, HS)]),
             (f"a2a{far}2", WKV.at[y, zz, :, pl.ds(HS, HS)]))
    send(is0,
         ("wq_r", WQ.at[y], WQ.at[y], {"dp": at_yr}),
         ("wq_l", WQ.at[y], WQ.at[y], {"dp": at_yl}),
         ("wk_r", WKV.at[y], WKV.at[y], {"dp": at_yr}),
         ("wk_l", WKV.at[y], WKV.at[y], {"dp": at_yl}),
         ("wq_c", WQ.at[y], WQ.at[y], {"section": 1}),
         ("wk_c", WKV.at[y], WKV.at[y], {"section": 1}))

    @pl.when(is1)
    def _():
        for c in local1:
            c.wait()

    kv_mine = WKV1.at[y, z]
    send(is1,
         ("q1", WQ1, WQ1, {"section": 0}),
         ("o1", WO1, WO1, {"section": 0}))
    ring_z2("n", N)
    send(is1,
         ("k1r", kv_mine, kv_mine, {"dp": at_zr}),
         ("k1l", kv_mine, kv_mine, {"dp": at_zl}))

    def wo_half(yy, half):
        return WO.at[pl.ds(pl.multiple_of(yy * HS + half * 64, 64), 64)]

    def two(ref, yy, half):
        return ref.at[yy, pl.ds(2 * half, 2)]

    recv(is0, ("wo_r", wo_rows(yl)))
    send(is0, ("wo_R", wo_half(yl, 0), wo_half(yl, 0), {"dp": at_yr}),
         ("wo_cl", wo_rows(yl), wo_rows(yl), {"section": 1}))
    recv(is0, ("wo_l", wo_rows(yr)))
    send(is0, ("wo_L", wo_half(yr, 1), wo_half(yr, 1), {"dp": at_yl}),
         ("wo_cr", wo_rows(yr), wo_rows(yr), {"section": 1}))
    k1_half = lambda yy, zz, half: WKV1.at[yy, zz, pl.ds(half * 128, 128)]
    recv(is1, ("k1r", WKV1.at[y, zl]))
    send(is1, ("k1R", k1_half(y, zl, 0), k1_half(y, zl, 0), {"dp": at_zr}))
    recv(is1, ("k1l", WKV1.at[y, zr]))
    send(is1, ("k1L", k1_half(y, zr, 1), k1_half(y, zr, 1), {"dp": at_zl}))

    QA[...] = jnp.zeros_like(QA)
    KVA[...] = jnp.zeros_like(KVA)

    def project(yy):
        @pl.loop(0, RING)
        def _(zz):
            block = N[:, pl.ds(pl.multiple_of((zz * RING + yy) * BLK, BLK), BLK)]
            QA[...] += mm(block, WQ[yy, zz])
            KVA[...] += mm(block, WKV[yy, zz])

    ring_z3("n", N)
    recv(is1, ("wq_c", WQ.at[y]), ("wk_c", WKV.at[y]))
    project(y)
    for tag, yy, fwd, half, at, back in (("r", yl, "R", 0, at_yr, "cl"), ("l", yr, "L", 1, at_yl, "cr")):
        recv(is0, ("wq_" + tag, WQ.at[yy]), ("wk_" + tag, WKV.at[yy]))
        send(is0,
             ("wq_" + fwd, two(WQ, yy, half), two(WQ, yy, half), {"dp": at}),
             ("wk_" + fwd, two(WKV, yy, half), two(WKV, yy, half), {"dp": at}),
             ("wq_" + back, WQ.at[yy], WQ.at[yy], {"section": 1}),
             ("wk_" + back, WKV.at[yy], WKV.at[yy], {"section": 1}))
    for back, yy in (("cl", yl), ("cr", yr)):
        recv(is1, ("wq_" + back, WQ.at[yy]), ("wk_" + back, WKV.at[yy]))
        project(yy)
    recv(is0, ("wo_R", wo_half(yo, 0)), ("wo_L", wo_half(yo, 1)))
    send(is0, ("wo_co", wo_rows(yo), wo_rows(yo), {"section": 1}))
    recv(is0, ("wq_R", two(WQ, yo, 0)), ("wk_R", two(WKV, yo, 0)),
         ("wq_L", two(WQ, yo, 1)), ("wk_L", two(WKV, yo, 1)))
    send(is0, ("wq_co", WQ.at[yo], WQ.at[yo], {"section": 1}),
         ("wk_co", WKV.at[yo], WKV.at[yo], {"section": 1}))
    recv(is1, ("wq_co", WQ.at[yo]), ("wk_co", WKV.at[yo]))
    recv(is1, ("k1R", k1_half(y, zo, 0)), ("k1L", k1_half(y, zo, 1)))
    send(is1,
         ("k1yr", WKV1.at[y], WKV1.at[y], {"dp": at_yr}),
         ("k1yl", WKV1.at[y], WKV1.at[y], {"dp": at_yl}),
         ("k1c", WKV1.at[y], WKV1.at[y], {"section": 0}))
    project(yo)
    QB[...] = QA[...].astype(BF16)
    KVB[...] = KVA[...].astype(BF16)

    r_i = lax.broadcasted_iota(jnp.int32, (ROWS, ROWS), 0)
    c_i = lax.broadcasted_iota(jnp.int32, (ROWS, ROWS), 1)
    seen = jnp.logical_and(r_i // SEQ == c_i // SEQ, c_i <= r_i)
    for h in range(GROUP):
        span = slice(h * HS, (h + 1) * HS)
        logits = nt(QB[:, span], KVB[:, :HS]) * SCALE
        grown = jnp.where(seen, jnp.exp(jnp.where(seen, logits, 0.0)), 0.0)
        weights = grown / jnp.sum(grown, -1, keepdims=True)
        WA[h] = weights
        context = mm(weights.astype(BF16), KVB[:, HS:])
        CTX[:, span] = context.astype(BF16)
        CTT[span, :] = context.T.astype(BF16)
    send(None, ("ctt", CTT, CTP, {"section": other}))

    recv(is1, ("wo_c", wo_rows(y)), ("wo_cl", wo_rows(yl)), ("wo_cr", wo_rows(yr)), ("wo_co", wo_rows(yo)))

    @pl.loop(0, 8)
    def _(t):
        span = pl.ds(pl.multiple_of(t * 512, 512), 512)
        OP[:, span] = mm(CTX[...], WO[:, span]).astype(BF16)

    send(None, ("o1r", half_rows(OP, zo, 0), FWD.at[0], {"dp": at_zr}),
         ("o1l", half_rows(OP, zo, 1), FWD.at[1], {"dp": at_zl}))
    for side, tag, dest, at in ((0, "o1r", zr, at_zr), (1, "o1l", zl, at_zl)):
        recv(None, (tag, FWD.at[side]))

        @pl.loop(0, 2)
        def _(g):
            rows = pl.ds(pl.multiple_of(dest * SEQ + side * 32 + g * 16, 16), 16)
            part = pl.ds(pl.multiple_of(g * 16, 16), 16)
            OP[rows, :] = (OP[rows, :].astype(F32) + FWD[side, part, :].astype(F32)).astype(BF16)

        send(None, (f"o2{side}", OP.at[my_rows(dest)], LAND.at[side], {"dp": at}))

    for tag, yy, fwd, half, at in (("r", yl, "R", 0, at_yr), ("l", yr, "L", 1, at_yl)):
        recv(is1, ("k1y" + tag, WKV1.at[yy]))
        send(is1, ("k1y" + fwd, two(WKV1, yy, half), two(WKV1, yy, half), {"dp": at}),
             ("k1c" + tag, WKV1.at[yy], WKV1.at[yy], {"section": 0}))

    recv(None, ("o20", LAND.at[0]), ("o21", LAND.at[1]))

    length = jnp.where(is0, lens[0, 0], lens[0, 1])
    NL[...] = jnp.zeros_like(NL)
    HL[...] = jnp.zeros_like(HL)

    def last_rows(g):
        return lax.broadcasted_iota(jnp.int32, (16, D), 0) + g * 16 == length - 1

    @pl.loop(0, 4)
    def _(g):
        part = pl.ds(pl.multiple_of(g * 16, 16), 16)
        own = pl.ds(pl.multiple_of(z * SEQ + g * 16, 16), 16)
        total = X[part, :].astype(F32) + (
            OP[own, :].astype(F32) + LAND[0, part, :].astype(F32) + LAND[1, part, :].astype(F32)
        )
        hidden = total.astype(BF16)
        H1[part, :] = hidden
        rows = hidden.astype(F32)
        unit = rows * lax.rsqrt(jnp.mean(rows * rows, -1, keepdims=True) + EPS)
        normed = (unit * GA[1]).astype(BF16)
        N1[part, :] = normed
        last = last_rows(g)
        NL[...] += jnp.sum(jnp.where(last, normed.astype(F32), 0.0), 0, keepdims=True)
        HL[...] += jnp.sum(jnp.where(last, rows, 0.0), 0, keepdims=True)

    for j in range(N_DP):
        S1[j] = NL[:, j * BLK : (j + 1) * BLK]
    exchange("e1", lambda peer, slot: S1.at[peer], R1)
    R1[N_DP - 1] = S1[dp]
    KVA1[...] = jnp.zeros_like(KVA1)

    def project1(yy):
        @pl.loop(0, RING)
        def _(zz):
            block = N1[:, pl.ds(pl.multiple_of((zz * RING + yy) * BLK, BLK), BLK)]
            KVA1[...] += mm(block, WKV1[yy, zz])

    recv(is0, ("q1", WQ1), ("o1", WO1), ("k1c", WKV1.at[y]))
    project1(y)
    landed("e1", R1)
    for j in range(N_DP):
        X1[j : j + 1, :] = R1[j]
    back = mm(X1[...].astype(BF16), WQ1[...])
    for j in range(N_DP):
        T2[j] = back[j : j + 1, :]
    exchange("e2", lambda peer, slot: T2.at[slot], R2)
    R2[N_DP - 1] = T2[N_DP - 1]
    for tag, yy in (("r", yl), ("l", yr)):
        recv(is0, ("k1c" + tag, WKV1.at[yy]))
        project1(yy)
    recv(is1, ("k1yR", two(WKV1, yo, 0)), ("k1yL", two(WKV1, yo, 1)))
    send(is1, ("k1co", WKV1.at[yo], WKV1.at[yo], {"section": 0}))
    recv(is0, ("k1co", WKV1.at[yo]))
    project1(yo)
    for g in range(RING):
        KC[g * SEQ : (g + 1) * SEQ, :] = KVA1[:, g * HS : (g + 1) * HS].astype(BF16)
        VC[g * SEQ : (g + 1) * SEQ, :] = KVA1[:, (RING + g) * HS : (RING + g + 1) * HS].astype(BF16)
    landed("e2", R2)
    q_row = R2[0]
    for j in range(1, N_DP):
        q_row = q_row + R2[j]
    for h in range(HEADS):
        Q16[h : h + 1, :] = q_row[:, h * HS : (h + 1) * HS]
    q_last = Q16[...].astype(BF16)

    h_i = lax.broadcasted_iota(jnp.int32, (HEADS, RING * SEQ), 0)
    k_i = lax.broadcasted_iota(jnp.int32, (HEADS, RING * SEQ), 1)
    seen1 = jnp.logical_and(h_i // GROUP == k_i // SEQ, k_i % SEQ < length)
    logits = nt(q_last, KC[...]) * SCALE
    grown = jnp.where(seen1, jnp.exp(jnp.where(seen1, logits, 0.0)), 0.0)
    weights1 = grown / jnp.sum(grown, -1, keepdims=True)
    probs1 = weights1.astype(BF16)
    context1 = mm(probs1, VC[...]).astype(BF16).astype(F32)
    for h in range(HEADS):
        S3[h] = context1[h : h + 1, :]
    exchange("e3", lambda peer, slot: S3.at[peer], R3)
    R3[N_DP - 1] = S3[dp]
    landed("e3", R3)
    for j in range(N_DP):
        X3[j : j + 1, :] = R3[j]
    x3 = X3[...].astype(BF16)
    for t in range(4):
        back = mm(x3, WO1[:, t * 1024 : (t + 1) * 1024])
        for j in range(N_DP):
            T4[j, :, t * 1024 : (t + 1) * 1024] = back[j : j + 1, :]
    exchange("e4", lambda peer, slot: T4.at[slot], R4)
    R4[N_DP - 1] = T4[N_DP - 1]
    landed("e4", R4)
    update = R4[0]
    for j in range(1, N_DP):
        update = update + R4[j]
    final = (HL[...] + update).astype(BF16).astype(F32)

    scale1 = lax.rsqrt(jnp.mean(final * final, -1, keepdims=True) + EPS)
    unit1 = final * scale1
    weighed = unit1 * HD[...]
    score = jnp.sum(weighed, -1, keepdims=True)
    mine_sc = m * 2 + s
    SCB[mine_sc] = jnp.broadcast_to(score, (1, HS))
    send(None, *[
        (f"sc{dm}{ds}", SCB.at[mine_sc], SCB.at[mine_sc], {"member": (m + dm) % 4, "section": (s + ds) % 2})
        for dm in range(4) for ds in range(2) if dm or ds
    ])
    toward = scale1 * (HD[...] - unit1 * (score / D))
    S6[...] = toward.astype(BF16).astype(F32)
    exchange("e6", lambda peer, slot: S6, R6)
    R6[N_DP - 1] = S6[...]
    recv(None, *[
        (f"sc{dm}{ds}", SCB.at[((m + 4 - dm) % 4) * 2 + (s + ds) % 2])
        for dm in range(4) for ds in range(2) if dm or ds
    ])
    chosen = (SCB[0] + SCB[2] + SCB[4] + SCB[6]) / 4
    rejected = (SCB[1] + SCB[3] + SCB[5] + SCB[7]) / 4
    spread = jax.nn.sigmoid(rejected - chosen)
    direction = jnp.where(is0, -spread, spread)
    landed("e6", R6)
    for j in range(N_DP):
        X6[j : j + 1, :] = R6[j]
    back = jnp.zeros((N_DP, HS), F32)
    for t in range(4):
        span = slice(t * 1024, (t + 1) * 1024)
        back = back + nt(X6[:, span].astype(BF16), WO1[:, span])
    for j in range(N_DP):
        T7[j] = back[j : j + 1, :]
    exchange("e7", lambda peer, slot: T7.at[slot], R7)
    R7[N_DP - 1] = T7[N_DP - 1]
    landed("e7", R7)
    for h in range(HEADS):
        DC[h : h + 1, :] = R7[slot_of(h)]
    d_ctx = (DC[...] * direction).astype(BF16)
    d_probs = nt(d_ctx, VC[...])
    leaned = weights1 * d_probs
    d_logits = (leaned - weights1 * jnp.sum(leaned, -1, keepdims=True)) * SCALE
    d_logits = d_logits.astype(BF16)
    d_query = mm(d_logits, KC[...]).astype(BF16).astype(F32)
    for h in range(HEADS):
        S8[:, h * HS : (h + 1) * HS] = d_query[h : h + 1, :]
    lane = lax.broadcasted_iota(jnp.int32, (1, HS), 1)
    meta = jnp.where(lane == 0, direction, jnp.where(lane == 1, chosen, rejected))
    S8[:, HEADS * HS :] = jnp.where(lane == 3, route[0].astype(F32), meta)
    exchange("e8", lambda peer, slot: S8, R8)
    R8[N_DP - 1] = S8[...]
    d_key = tn(d_logits, q_last)
    d_value = tn(probs1, d_ctx)
    for g in range(RING):
        DKV[:, g * HS : (g + 1) * HS] = d_key[g * SEQ : (g + 1) * SEQ, :].astype(BF16)
        DKV[:, (RING + g) * HS : (RING + g + 1) * HS] = d_value[g * SEQ : (g + 1) * SEQ, :].astype(BF16)

    @pl.loop(0, N_DP)
    def _(j):
        span = pl.ds(pl.multiple_of(j * BLK, BLK), BLK)
        GN[:, span] = nt(DKV[...], WKV1[j % RING, j // RING])

    landed("e8", R8)
    for j in range(N_DP):
        X8[j : j + 1, :] = R8[j, :, : HEADS * HS]
    back = nt(X8[...].astype(BF16), WQ1[...])
    for j in range(N_DP):
        T9[j] = back[j : j + 1, :]
    exchange("e9", lambda peer, slot: T9.at[slot], R9)
    R9[N_DP - 1] = T9[N_DP - 1]
    answer = jnp.zeros((1, HS), F32)
    for j in range(N_DP):
        extra = R8[j, :, HEADS * HS :]
        answer = answer + jnp.where(extra[:, 3:4] == dp.astype(F32), extra, 0.0)
        GC[s, j : j + 1, :] = R6[j] * extra[:, 0:1]
    scores_out[...] = answer[:, 1:3]
    XC[s] = X3[...]
    send(is0, ("xc", XC.at[0], XC.at[0], {"section": 1}), ("gc", GC.at[0], GC.at[0], {"section": 1}))
    landed("e9", R9)
    for h in range(N_DP):
        GNL[:, h * BLK : (h + 1) * BLK] = R9[slot_of(h)]

    HL[...] = (toward * direction[:, 0:1]).astype(BF16).astype(F32)
    NL[...] = jnp.zeros_like(NL)

    @pl.loop(0, 4)
    def _(g):
        part = pl.ds(pl.multiple_of(g * 16, 16), 16)
        rows = H1[part, :].astype(F32)
        scale = lax.rsqrt(jnp.mean(rows * rows, -1, keepdims=True) + EPS)
        unit = rows * scale
        last = last_rows(g)
        d_normed = GN[part, :] + jnp.where(last, GNL[...], 0.0)
        NL[...] += jnp.sum(d_normed * unit, 0, keepdims=True)
        pulled = d_normed * GA[1]
        d_rows = scale * (pulled - unit * jnp.mean(pulled * unit, -1, keepdims=True))
        G[pl.ds(pl.multiple_of(z * SEQ + g * 16, 16), 16), :] = (
            d_rows + jnp.where(last, HL[...], 0.0)
        ).astype(BF16)

    ring_z1("g", G)
    across = pl.ds(pl.multiple_of(other * HALF, HALF), HALF)

    def to_core(tag, zz):
        send(None, (tag, G.at[my_rows(zz), across], GP.at[my_rows(zz)], {"section": other}))

    to_core("gp0", z)

    recv(is1, ("xc", XC.at[0]), ("gc", GC.at[0]))

    @pl.when(is1)
    def _():
        rows_a, rows_b = XC[0].astype(BF16), XC[1].astype(BF16)

        @pl.loop(0, 8)
        def _(t):
            span = pl.ds(pl.multiple_of(t * 512, 512), 512)
            grad_out[0, 0, :, span] = tn(rows_a, GC[0, :, span].astype(BF16)) + tn(
                rows_b, GC[1, :, span].astype(BF16)
            )

    for h in range(N_DP):
        SG[h, :, BLK:] = NL[:, h * BLK : (h + 1) * BLK]

    ring_z2("g", G)
    to_core("gp1", zl)
    to_core("gp2", zr)
    ring_z3("g", G)
    to_core("gp3", zo)

    recv(None, ("ctt", CTP), ("gp0", GP.at[my_rows(z)]), ("gp1", GP.at[my_rows(zl)]),
         ("gp2", GP.at[my_rows(zr)]), ("gp3", GP.at[my_rows(zo)]))

    @pl.loop(0, 4)
    def _(t):
        span = pl.ds(pl.multiple_of(t * 512, 512), 512)
        here = pl.ds(pl.multiple_of(s * HALF + t * 512, 512), 512)
        GOP[:, span] = (mm(CTT[...], G[:, here]) + mm(CTP[...], GP[:, span])).astype(BF16)

    def head_rows(yy):
        return GOP.at[pl.ds(pl.multiple_of(yy * HS, HS), HS)]

    def head_half(yy, half):
        return GOP.at[pl.ds(pl.multiple_of(yy * HS + half * 64, 64), 64)]

    send(None, ("r1r", head_half(yo, 0), FWD2.at[0], {"dp": at_yr}),
         ("r1l", head_half(yo, 1), FWD2.at[1], {"dp": at_yl}))
    send(is1, ("rc", head_rows(y), LAND2.at[4], {"section": 0}))

    DCT[...] = jnp.zeros_like(DCT)

    @pl.loop(0, 8)
    def _(t):
        span = pl.ds(pl.multiple_of(t * 512, 512), 512)
        DCT[...] += nt(G[:, span], WO[:, span])

    for side, tag, dest, at in ((0, "r1r", yr, at_yr), (1, "r1l", yl, at_yl)):
        recv(None, (tag, FWD2.at[side]))
        rows = pl.ds(pl.multiple_of(dest * HS + side * 64, 64), 64)
        GOP[rows, :] = (GOP[rows, :].astype(F32) + FWD2[side].astype(F32)).astype(BF16)
        send(is0, (f"ra{side}", head_rows(dest), LAND2.at[side], {"dp": at, "section": 0}))
        send(is1, (f"rb{side}", head_rows(dest), LAND2.at[2 + side], {"dp": at, "section": 0}))

    d_key = jnp.zeros((ROWS, HS), F32)
    d_value = jnp.zeros((ROWS, HS), F32)
    for h in range(GROUP):
        span = slice(h * HS, (h + 1) * HS)
        d_ctx = DCT[:, span].astype(BF16)
        weights = WA[h]
        leaned = weights * nt(d_ctx, KVB[:, HS:])
        d_logits = (leaned - weights * jnp.sum(leaned, -1, keepdims=True)) * SCALE
        d_logits = d_logits.astype(BF16)
        DQB[:, span] = mm(d_logits, KVB[:, :HS]).astype(BF16)
        d_key = d_key + tn(d_logits, QB[:, span])
        d_value = d_value + tn(weights.astype(BF16), d_ctx)
    DKVB[:, :HS] = d_key.astype(BF16)
    DKVB[:, HS:] = d_value.astype(BF16)

    @pl.loop(0, N_DP)
    def _(j):
        span = pl.ds(pl.multiple_of(j * BLK, BLK), BLK)
        yy, zz = j % RING, j // RING
        d_normed = nt(DQB[...], WQ[yy, zz]) + nt(DKVB[...], WKV[yy, zz])
        sums = jnp.sum(d_normed * N[:, span].astype(F32), 0, keepdims=True)
        SG[j, :, :BLK] = sums / GA[0, :, span]

    exchange("e10", lambda peer, slot: SG.at[peer], RG)
    RG[N_DP - 1] = SG[dp]
    landed("e10", RG)
    total = RG[0]
    for j in range(1, N_DP):
        total = total + RG[j]
    SP[...] = total
    send(None, ("sp", SP, PG, {"section": other}))

    recv(is0, ("rc", LAND2.at[4]), ("ra0", LAND2.at[0]), ("ra1", LAND2.at[1]),
         ("rb0", LAND2.at[2]), ("rb1", LAND2.at[3]))
    recv(None, ("sp", PG))
    both = total + PG[...]
    gain_out[0] = jnp.where(is0, both[:, :BLK], both[:, BLK:])

    @pl.when(is0)
    def _():
        @pl.loop(0, 8)
        def _(g):
            part = pl.ds(pl.multiple_of(g * 16, 16), 16)
            own = pl.ds(pl.multiple_of(y * HS + g * 16, 16), 16)
            grad_out[0, 0, part, pl.ds(0, HALF)] = GOP[own, :].astype(F32) + (
                LAND2[0, part, :].astype(F32) + LAND2[1, part, :].astype(F32)
            )
            grad_out[0, 0, part, pl.ds(HALF, HALF)] = LAND2[4, part, :].astype(F32) + (
                LAND2[2, part, :].astype(F32) + LAND2[3, part, :].astype(F32)
            )

    for cond, fin in pending:
        guarded(cond, fin)
    assert len(ids) <= N_SEMS, len(ids)


def body(embeds, lengths, route, w_query, w_keyval, w_out, norm_gain, head):
    hbm = pl.BlockSpec(memory_space=pl.ANY)
    vmem = pl.BlockSpec(memory_space=pltpu.VMEM)
    smem = pl.BlockSpec(memory_space=pltpu.SMEM)
    V = pltpu.VMEM
    row = lambda n: V((1, n), F32)
    slots = lambda n: V((N_DP, 1, n), F32)
    scratch = [
        V((SEQ, D), BF16), V((2, 1, D), F32), row(D), V((ROWS, D), BF16),
        V((RING, RING, BLK, QW), BF16), V((RING, RING, BLK, 2 * HS), BF16), V((QW, D), BF16),
        V((BLK, HEADS * HS), BF16), V((HS, D), BF16), V((RING, RING, BLK, 2 * RING * HS), BF16),
        V((ROWS, QW), F32), V((ROWS, 2 * HS), F32), V((ROWS, QW), BF16), V((ROWS, 2 * HS), BF16),
        V((GROUP, ROWS, ROWS), F32), V((ROWS, QW), BF16), V((QW, ROWS), BF16), V((QW, ROWS), BF16),
        V((ROWS, D), BF16), V((2, 32, D), BF16), V((2, SEQ, D), BF16),
        V((SEQ, D), BF16), V((SEQ, D), BF16), V((SEQ, 2 * RING * HS), F32),
        V((RING * SEQ, HS), BF16), V((RING * SEQ, HS), BF16), V((HEADS, HS), F32),
        row(D), row(D), slots(BLK), slots(BLK), V((N_DP, BLK), F32), slots(HEADS * HS), slots(HEADS * HS),
        slots(HS), slots(HS), V((N_DP, HS), F32), slots(D), slots(D), V((8, 1, HS), F32),
        row(D), slots(D), V((N_DP, D), F32), slots(HS), slots(HS), V((HEADS, HS), F32),
        row(HEADS * HS + HS), slots(HEADS * HS + HS), V((N_DP, HEADS * HS), F32), slots(BLK), slots(BLK),
        row(D), V((2, N_DP, HS), F32), V((2, N_DP, D), F32), V((SEQ, D), F32), V((SEQ, 2 * RING * HS), BF16),
        V((ROWS, D), BF16), V((ROWS, HALF), BF16), V((ROWS, QW), F32), V((ROWS, QW), BF16),
        V((ROWS, 2 * HS), BF16), V((QW, HALF), BF16), V((2, 64, HALF), BF16), V((5, HS, HALF), BF16),
        slots(2 * BLK), slots(2 * BLK), row(2 * BLK), row(2 * BLK),
        pltpu.SemaphoreType.DMA((N_SEMS,)), pltpu.SemaphoreType.DMA((N_SEMS,)), pltpu.SemaphoreType.DMA((8,)),
    ]
    return pl.pallas_call(
        kernel,
        out_shape=(
            jax.ShapeDtypeStruct((1, 2), F32),
            jax.ShapeDtypeStruct((1, 1, HS, D), F32),
            jax.ShapeDtypeStruct((1, 1, BLK), F32),
        ),
        in_specs=[hbm, smem, smem, hbm, hbm, hbm, hbm, hbm],
        out_specs=(vmem, vmem, vmem),
        scratch_shapes=scratch,
        compiler_params=pltpu.CompilerParams(
            collective_id=0, has_side_effects=True, vmem_limit_bytes=60 * 1024 * 1024
        ),
    )(embeds, lengths, route, w_query, w_keyval, w_out, norm_gain, head)


def solution(mesh):
    placed = (
        P("member", "dp", None, None, None),
        P("dp", None),
        P("dp"),
        P("member", "section", "dp", None),
        P("member", "section", "dp", None),
        P("member", "section", "dp", None),
        P("member", "section", None),
        P("member", None),
    )
    return jax.shard_map(
        body,
        mesh=mesh,
        in_specs=placed,
        out_specs=(P("dp", None), P("member", "section", "dp", None), P("member", "section", "dp")),
        check_vma=False,
    )
```

time: 786 us -> 200 us (0.25); the launches traced: 774 us -> 199 us
  waiting for transfers between devices: 540 us -> 0 us
  Pallas kernels: 0 us -> 193 us
  matrix products: 102 us -> 0 us
  blocking collectives: 75.4 us -> 0 us
  other arithmetic: 17.5 us -> 0 us
  between operations: 17.3 us -> 1.29 us
  local copies, waits for them, and re-layouts: 18.1 us -> 4.76 us
    all_gather x4 -> x0, waiting for transfers between devices: 448 us -> none  [the longest x1 182 us: body(): lax.all_gather(flat_pairs, 'dp', axis=0, tiled=True)]
    pallas_call x0 -> x1, Pallas kernels: none -> 193 us  [body(): pl.pallas_call(kernel, out_shape=(jax.ShapeDtypeStruct((1, 2), F32), jax....]
    dot_general x15 -> x0, matrix products: 102 us -> none  [the longest x1 32.2 us: body(): jnp.dot(selector, lax.all_gather(flat_pairs, 'dp', axis=0, tiled=True), p...]
    reduce_scatter x1 -> x0, waiting for transfers between devices: 73.8 us -> none  [body(): lax.psum_scatter(out_term.astype(jnp.bfloat16), 'dp', scatter_dimension=0...]
    unnamed x2 -> x0, blocking collectives: 48 us -> none
    all_gather x1 -> x0, blocking collectives: 15.7 us -> none  [body(): lax.all_gather(lengths, 'dp', axis=0, tiled=True)]
    ppermute x2 -> x0, waiting for transfers between devices: 15.7 us -> none  [from_behind(): lax.ppermute(value, axis, [(source, source + steps) for source in range(f...]
    psum x1 -> x0, blocking collectives: 11.6 us -> none  [body(): totals = lax.psum(own_scores, ('member', 'section'))]
  transfers between devices with their start and end apart: 7 -> 0, of which waited for: 7 -> 0; matrix products, arithmetic and copies ran while one was open for 5% -> 0% of each run, Pallas kernels for 0% -> 0%
where the time goes in v1:
time: 200 us; the launch traced here: 199 us
  Pallas kernels  193 us (96%)
  local copies, waits for them, and re-layouts  4.76 us (2%)
    pallas_call x1, Pallas kernels, body(): pl.pallas_call(kernel, out_shape=(jax.ShapeDtypeStruct((1, 2), F32), jax....  193 us
    unnamed x5, local copies, waits for them, and re-layouts  4.76 us

profile of v1, /device:TPU:1, one launch (start us, length us, event | category | flops | bytes accessed | tf_op | source)
XLA Modules:
  0.0 199.4 jit_solution(6819941218411380766)
XLA Ops:
  1.3 193.3 %shard_map.103 = (f32[1,2]{1,0:T(1,128)}, f32[1,1,128,4096]{3,2,1,0:T(8,128)}, f32[1,1,256]{2,1,0:T(1,128)}) custom-call(bf16[1,1,2,64,4096]{4,3,2,1,0:T(8,128)(2,1)} %emb.1, s32[1,2]{1,0:T(1,128)} %lens.1, s32[1]{0:T(128)S(6)} %copy.14.route, bf16[1,1,256,2048]{3,2,1,0:T(8,128)(2,1)} %wq.1, bf16[1,1,256,1024]{3,2,1,0:T(8,128)(2,1)} %wkv.1, ...), custom_call_target="tpu_custom_call" | custom-call | tf_op jit(solution)/shard_map/pallas_call | solution.py:684
  194.6 1.1 copy.15
  195.7 0.0 copy-start
  195.7 3.1 %copy.16 = f32[1,1,128,4096]{3,2,1,0:T(8,128)} copy(f32[1,1,128,4096]{3,2,1,0:T(8,128)} %get-tuple-element.7) | data formatting | bytes 4194304
  198.8 0.0 copy-done
  198.8 0.6 copy.17
Async XLA Ops:
  195.7 3.1 %copy-start = (f32[1,1,256]{2,1,0:T(1,128)S(1)}, f32[1,1,256]{2,1,0:T(1,128)}, u32[]{:S(2)}) copy-start(f32[1,1,256]{2,1,0:T(1,128)} %get-tuple-element.8) | copy-start | bytes 3076

commit v2 on v1

--- a/solution.py
+++ b/solution.py
@@ -21,7 +21,7 @@
 BLK = D // N_DP
 HALF = D // 2
 SCALE = HS ** (-0.5)
-N_SEMS = 112
+N_SEMS = 160
 
 
 def mm(a, b):
@@ -39,12 +39,12 @@
 def kernel(
     emb, lens, route, wq, wkv, wo, gain, head,
     scores_out, grad_out, gain_out,
-    X, GA, HD, N, WQ, WKV, WO, WQ1, WO1, WKV1,
-    QA, KVA, QB, KVB, WA, CTX, CTT, CTP, OP, FWD, LAND,
+    X, GA, HD, N, W, WO, WQ1, WO1, WKV1,
+    QA, QB, WA, CTX, CTT, CTP, OP, FWD, LAND,
     H1, N1, KVA1, KC, VC, Q16,
     NL, HL, S1, R1, X1, T2, R2, S3, R3, X3, T4, R4, SCB, S6, R6, X6, T7, R7, DC,
     S8, R8, X8, T9, R9, GNL, XC, GC, GN, DKV,
-    G, GP, DCT, DQB, DKVB, GOP, FWD2, LAND2, SG, RG, SP, PG,
+    G, GP, DCT, DQB, GOP, FWD2, LAND2, SG, RG, SP, PG,
     ssem, rsem, lsem,
 ):
     s = lax.axis_index("section")
@@ -133,9 +133,9 @@
 
     def slices(dest_z):
         return (
-            (cols(wq_mine, dest_z * QW, QW), WQ.at[y, z]),
-            (cols(wkv_mine, dest_z * HS, HS), WKV.at[y, z, :, pl.ds(0, HS)]),
-            (cols(wkv_mine, RING * HS + dest_z * HS, HS), WKV.at[y, z, :, pl.ds(HS, HS)]),
+            (cols(wq_mine, dest_z * QW, QW), W.at[y, z, :, pl.ds(0, QW)]),
+            (cols(wkv_mine, dest_z * HS, HS), W.at[y, z, :, pl.ds(QW, HS)]),
+            (cols(wkv_mine, RING * HS + dest_z * HS, HS), W.at[y, z, :, pl.ds(QW + HS, HS)]),
         )
 
     wo_rows = lambda yy: WO.at[pl.ds(pl.multiple_of(yy * HS, HS), HS)]
@@ -177,11 +177,26 @@
     for far, at in ((1, at_zr), (3, at_zl), (2, at_zo)):
         dest = (z + far) % RING
         send(is0, *[(f"a2a{far}{n}", a, b, {"dp": at}) for n, (a, b) in enumerate(slices(dest))])
-    mine = wo_rows(y)
-    send(is0,
-         ("wo_r", wo_mine, mine, {"dp": at_yr}),
-         ("wo_l", wo_mine, mine, {"dp": at_yl}),
-         ("wo_c", wo_mine, mine, {"section": 1}))
+
+    def w_out_step(zz, n):
+        chunk = W.at[y, zz]
+        send(is0, (f"w{n}r", chunk, chunk, {"dp": at_yr}), (f"w{n}l", chunk, chunk, {"dp": at_yl}),
+             (f"w{n}c", chunk, chunk, {"section": 1}))
+
+    @pl.when(is0)
+    def _():
+        for c in local0:
+            c.wait()
+
+    @pl.when(is1)
+    def _():
+        for c in local1:
+            c.wait()
+
+    w_out_step(z, 0)
+    LO, HI = pl.ds(0, 128), pl.ds(128, 128)
+    b_own = WKV1.at[y, z, HI]
+    send(is1, ("byr", b_own, b_own, {"dp": at_yr}), ("byl", b_own, b_own, {"dp": at_yl}))
     send(None, ("gain", gain.at[0], GA.at[s], {"section": other}))
 
     lx.wait()
@@ -217,108 +232,109 @@
 
     ring_z1("n", N)
 
-    @pl.when(is0)
-    def _():
-        for c in local0:
-            c.wait()
-
-    for far, zz in ((1, zl), (3, zr), (2, zo)):
-        recv(is0, (f"a2a{far}0", WQ.at[y, zz]),
-             (f"a2a{far}1", WKV.at[y, zz, :, pl.ds(0, HS)]),
-             (f"a2a{far}2", WKV.at[y, zz, :, pl.ds(HS, HS)]))
+    order = (z, zl, zr, zo)
+    for n, far in ((1, 1), (2, 3), (3, 2)):
+        zz = order[n]
+        recv(is0, (f"a2a{far}0", W.at[y, zz, :, pl.ds(0, QW)]),
+             (f"a2a{far}1", W.at[y, zz, :, pl.ds(QW, HS)]),
+             (f"a2a{far}2", W.at[y, zz, :, pl.ds(QW + HS, HS)]))
+        w_out_step(zz, n)
+    b_half = lambda yy, half: WKV1.at[yy, z, pl.ds(128 + 64 * half, 64)]
+    recv(is1, ("byr", WKV1.at[yl, z, HI]))
+    send(is1, ("byR", b_half(yl, 0), b_half(yl, 0), {"dp": at_yr}))
+    recv(is1, ("byl", WKV1.at[yr, z, HI]))
+    send(is1, ("byL", b_half(yr, 1), b_half(yr, 1), {"dp": at_yl}))
+    ring_z2("n", N)
+    a_own = WKV1.at[y, z, LO]
+    send(is1, ("azr", a_own, a_own, {"dp": at_zr}), ("azl", a_own, a_own, {"dp": at_zl}))
+    recv(is1, ("byR", b_half(yo, 0)), ("byL", b_half(yo, 1)))
+    b_item = lambda zz: WKV1.at[:, zz, HI]
+    send(is1, ("bzr", b_item(z), b_item(z), {"dp": at_zr}), ("bzl", b_item(z), b_item(z), {"dp": at_zl}),
+         ("bc", b_item(z), b_item(z), {"section": 0}))
+
+    for side, yy, fwd, at, kept in (("r", yl, "R", at_yr, (0, 2)), ("l", yr, "L", at_yl, (1, 3))):
+        for n in range(RING):
+            chunk = W.at[yy, order[n]]
+            recv(is0, (f"w{n}{side}", chunk))
+            if n in kept:
+                send(is0, (f"w{n}{fwd}", chunk, chunk, {"dp": at}))
+            send(is0, (f"w{n}c{side}", chunk, chunk, {"section": 1}))
+    mine = wo_rows(y)
     send(is0,
-         ("wq_r", WQ.at[y], WQ.at[y], {"dp": at_yr}),
-         ("wq_l", WQ.at[y], WQ.at[y], {"dp": at_yl}),
-         ("wk_r", WKV.at[y], WKV.at[y], {"dp": at_yr}),
-         ("wk_l", WKV.at[y], WKV.at[y], {"dp": at_yl}),
-         ("wq_c", WQ.at[y], WQ.at[y], {"section": 1}),
-         ("wk_c", WKV.at[y], WKV.at[y], {"section": 1}))
-
-    @pl.when(is1)
-    def _():
-        for c in local1:
-            c.wait()
-
-    kv_mine = WKV1.at[y, z]
-    send(is1,
-         ("q1", WQ1, WQ1, {"section": 0}),
-         ("o1", WO1, WO1, {"section": 0}))
-    ring_z2("n", N)
-    send(is1,
-         ("k1r", kv_mine, kv_mine, {"dp": at_zr}),
-         ("k1l", kv_mine, kv_mine, {"dp": at_zl}))
+         ("wo_r", mine, mine, {"dp": at_yr}),
+         ("wo_l", mine, mine, {"dp": at_yl}),
+         ("wo_c", mine, mine, {"section": 1}))
+
+    a_half = lambda zz, half: WKV1.at[y, zz, pl.ds(64 * half, 64)]
+    recv(is1, ("azr", WKV1.at[y, zl, LO]))
+    send(is1, ("azR", a_half(zl, 0), a_half(zl, 0), {"dp": at_zr}))
+    recv(is1, ("azl", WKV1.at[y, zr, LO]))
+    send(is1, ("azL", a_half(zr, 1), a_half(zr, 1), {"dp": at_zl}))
+
+    QA[...] = jnp.zeros_like(QA)
+
+    def project(yy):
+        @pl.loop(0, RING)
+        def _(zz):
+            block = N[:, pl.ds(pl.multiple_of((zz * RING + yy) * BLK, BLK), BLK)]
+            QA[...] += mm(block, W[yy, zz])
+
+    def w_core(tag, yy):
+        recv(is1, *[(f"w{n}c{tag}", W.at[yy, order[n]]) for n in range(RING)])
+
+    ring_z3("n", N)
+    w_core("", y)
+    project(y)
+    w_core("r", yl)
+    project(yl)
+    w_core("l", yr)
+    project(yr)
+    b_two = lambda zz, half: WKV1.at[pl.ds(2 * half, 2), zz, HI]
+    recv(is1, ("bzr", b_item(zl)))
+    send(is1, ("bzR", b_two(zl, 0), b_two(zl, 0), {"dp": at_zr}),
+         ("bcr", b_item(zl), b_item(zl), {"section": 0}))
+    recv(is1, ("bzl", b_item(zr)))
+    send(is1, ("bzL", b_two(zr, 1), b_two(zr, 1), {"dp": at_zl}),
+         ("bcl", b_item(zr), b_item(zr), {"section": 0}))
+    for n, fwd in ((0, "R"), (1, "L"), (2, "R"), (3, "L")):
+        chunk = W.at[yo, order[n]]
+        recv(is0, (f"w{n}{fwd}", chunk))
+        send(is0, (f"w{n}co", chunk, chunk, {"section": 1}))
 
     def wo_half(yy, half):
         return WO.at[pl.ds(pl.multiple_of(yy * HS + half * 64, 64), 64)]
 
-    def two(ref, yy, half):
-        return ref.at[yy, pl.ds(2 * half, 2)]
-
+    w_core("o", yo)
+    project(yo)
+    QB[...] = QA[...].astype(BF16)
     recv(is0, ("wo_r", wo_rows(yl)))
     send(is0, ("wo_R", wo_half(yl, 0), wo_half(yl, 0), {"dp": at_yr}),
          ("wo_cl", wo_rows(yl), wo_rows(yl), {"section": 1}))
     recv(is0, ("wo_l", wo_rows(yr)))
     send(is0, ("wo_L", wo_half(yr, 1), wo_half(yr, 1), {"dp": at_yl}),
          ("wo_cr", wo_rows(yr), wo_rows(yr), {"section": 1}))
-    k1_half = lambda yy, zz, half: WKV1.at[yy, zz, pl.ds(half * 128, 128)]
-    recv(is1, ("k1r", WKV1.at[y, zl]))
-    send(is1, ("k1R", k1_half(y, zl, 0), k1_half(y, zl, 0), {"dp": at_zr}))
-    recv(is1, ("k1l", WKV1.at[y, zr]))
-    send(is1, ("k1L", k1_half(y, zr, 1), k1_half(y, zr, 1), {"dp": at_zl}))
-
-    QA[...] = jnp.zeros_like(QA)
-    KVA[...] = jnp.zeros_like(KVA)
-
-    def project(yy):
-        @pl.loop(0, RING)
-        def _(zz):
-            block = N[:, pl.ds(pl.multiple_of((zz * RING + yy) * BLK, BLK), BLK)]
-            QA[...] += mm(block, WQ[yy, zz])
-            KVA[...] += mm(block, WKV[yy, zz])
-
-    ring_z3("n", N)
-    recv(is1, ("wq_c", WQ.at[y]), ("wk_c", WKV.at[y]))
-    project(y)
-    for tag, yy, fwd, half, at, back in (("r", yl, "R", 0, at_yr, "cl"), ("l", yr, "L", 1, at_yl, "cr")):
-        recv(is0, ("wq_" + tag, WQ.at[yy]), ("wk_" + tag, WKV.at[yy]))
-        send(is0,
-             ("wq_" + fwd, two(WQ, yy, half), two(WQ, yy, half), {"dp": at}),
-             ("wk_" + fwd, two(WKV, yy, half), two(WKV, yy, half), {"dp": at}),
-             ("wq_" + back, WQ.at[yy], WQ.at[yy], {"section": 1}),
-             ("wk_" + back, WKV.at[yy], WKV.at[yy], {"section": 1}))
-    for back, yy in (("cl", yl), ("cr", yr)):
-        recv(is1, ("wq_" + back, WQ.at[yy]), ("wk_" + back, WKV.at[yy]))
-        project(yy)
-    recv(is0, ("wo_R", wo_half(yo, 0)), ("wo_L", wo_half(yo, 1)))
-    send(is0, ("wo_co", wo_rows(yo), wo_rows(yo), {"section": 1}))
-    recv(is0, ("wq_R", two(WQ, yo, 0)), ("wk_R", two(WKV, yo, 0)),
-         ("wq_L", two(WQ, yo, 1)), ("wk_L", two(WKV, yo, 1)))
-    send(is0, ("wq_co", WQ.at[yo], WQ.at[yo], {"section": 1}),
-         ("wk_co", WKV.at[yo], WKV.at[yo], {"section": 1}))
-    recv(is1, ("wq_co", WQ.at[yo]), ("wk_co", WKV.at[yo]))
-    recv(is1, ("k1R", k1_half(y, zo, 0)), ("k1L", k1_half(y, zo, 1)))
-    send(is1,
-         ("k1yr", WKV1.at[y], WKV1.at[y], {"dp": at_yr}),
-         ("k1yl", WKV1.at[y], WKV1.at[y], {"dp": at_yl}),
-         ("k1c", WKV1.at[y], WKV1.at[y], {"section": 0}))
-    project(yo)
-    QB[...] = QA[...].astype(BF16)
-    KVB[...] = KVA[...].astype(BF16)
+    recv(is1, ("azR", a_half(zo, 0)), ("azL", a_half(zo, 1)))
+    a_item = lambda yy: WKV1.at[yy, :, LO]
+    send(is1, ("ayr", a_item(y), a_item(y), {"dp": at_yr}), ("ayl", a_item(y), a_item(y), {"dp": at_yl}),
+         ("ac", a_item(y), a_item(y), {"section": 0}))
 
     r_i = lax.broadcasted_iota(jnp.int32, (ROWS, ROWS), 0)
     c_i = lax.broadcasted_iota(jnp.int32, (ROWS, ROWS), 1)
     seen = jnp.logical_and(r_i // SEQ == c_i // SEQ, c_i <= r_i)
     for h in range(GROUP):
         span = slice(h * HS, (h + 1) * HS)
-        logits = nt(QB[:, span], KVB[:, :HS]) * SCALE
+        logits = nt(QB[:, span], QB[:, QW : QW + HS]) * SCALE
         grown = jnp.where(seen, jnp.exp(jnp.where(seen, logits, 0.0)), 0.0)
         weights = grown / jnp.sum(grown, -1, keepdims=True)
         WA[h] = weights
-        context = mm(weights.astype(BF16), KVB[:, HS:])
+        context = mm(weights.astype(BF16), QB[:, QW + HS :])
         CTX[:, span] = context.astype(BF16)
         CTT[span, :] = context.T.astype(BF16)
     send(None, ("ctt", CTT, CTP, {"section": other}))
-
+    send(is1, ("q1", WQ1, WQ1, {"section": 0}), ("o1", WO1, WO1, {"section": 0}))
+
+    recv(is0, ("wo_R", wo_half(yo, 0)), ("wo_L", wo_half(yo, 1)))
+    send(is0, ("wo_co", wo_rows(yo), wo_rows(yo), {"section": 1}))
     recv(is1, ("wo_c", wo_rows(y)), ("wo_cl", wo_rows(yl)), ("wo_cr", wo_rows(yr)), ("wo_co", wo_rows(yo)))
 
     @pl.loop(0, 8)
@@ -339,10 +355,13 @@
 
         send(None, (f"o2{side}", OP.at[my_rows(dest)], LAND.at[side], {"dp": at}))
 
+    a_two = lambda yy, half: WKV1.at[yy, pl.ds(2 * half, 2), LO]
+    recv(is1, ("bzR", b_two(zo, 0)), ("bzL", b_two(zo, 1)))
+    send(is1, ("bco", b_item(zo), b_item(zo), {"section": 0}))
     for tag, yy, fwd, half, at in (("r", yl, "R", 0, at_yr), ("l", yr, "L", 1, at_yl)):
-        recv(is1, ("k1y" + tag, WKV1.at[yy]))
-        send(is1, ("k1y" + fwd, two(WKV1, yy, half), two(WKV1, yy, half), {"dp": at}),
-             ("k1c" + tag, WKV1.at[yy], WKV1.at[yy], {"section": 0}))
+        recv(is1, ("ay" + tag, a_item(yy)))
+        send(is1, ("ay" + fwd, a_two(yy, half), a_two(yy, half), {"dp": at}),
+             ("ac" + tag, a_item(yy), a_item(yy), {"section": 0}))
 
     recv(None, ("o20", LAND.at[0]), ("o21", LAND.at[1]))
 
@@ -382,7 +401,8 @@
             block = N1[:, pl.ds(pl.multiple_of((zz * RING + yy) * BLK, BLK), BLK)]
             KVA1[...] += mm(block, WKV1[yy, zz])
 
-    recv(is0, ("q1", WQ1), ("o1", WO1), ("k1c", WKV1.at[y]))
+    recv(is0, ("q1", WQ1), ("o1", WO1), ("ac", a_item(y)),
+         ("bc", b_item(z)), ("bcr", b_item(zl)), ("bcl", b_item(zr)), ("bco", b_item(zo)))
     project1(y)
     landed("e1", R1)
     for j in range(N_DP):
@@ -393,11 +413,11 @@
     exchange("e2", lambda peer, slot: T2.at[slot], R2)
     R2[N_DP - 1] = T2[N_DP - 1]
     for tag, yy in (("r", yl), ("l", yr)):
-        recv(is0, ("k1c" + tag, WKV1.at[yy]))
+        recv(is0, ("ac" + tag, a_item(yy)))
         project1(yy)
-    recv(is1, ("k1yR", two(WKV1, yo, 0)), ("k1yL", two(WKV1, yo, 1)))
-    send(is1, ("k1co", WKV1.at[yo], WKV1.at[yo], {"section": 0}))
-    recv(is0, ("k1co", WKV1.at[yo]))
+    recv(is1, ("ayR", a_two(yo, 0)), ("ayL", a_two(yo, 1)))
+    send(is1, ("aco", a_item(yo), a_item(yo), {"section": 0}))
+    recv(is0, ("aco", a_item(yo)))
     project1(yo)
     for g in range(RING):
         KC[g * SEQ : (g + 1) * SEQ, :] = KVA1[:, g * HS : (g + 1) * HS].astype(BF16)
@@ -605,20 +625,20 @@
         span = slice(h * HS, (h + 1) * HS)
         d_ctx = DCT[:, span].astype(BF16)
         weights = WA[h]
-        leaned = weights * nt(d_ctx, KVB[:, HS:])
+        leaned = weights * nt(d_ctx, QB[:, QW + HS :])
         d_logits = (leaned - weights * jnp.sum(leaned, -1, keepdims=True)) * SCALE
         d_logits = d_logits.astype(BF16)
-        DQB[:, span] = mm(d_logits, KVB[:, :HS]).astype(BF16)
+        DQB[:, span] = mm(d_logits, QB[:, QW : QW + HS]).astype(BF16)
         d_key = d_key + tn(d_logits, QB[:, span])
         d_value = d_value + tn(weights.astype(BF16), d_ctx)
-    DKVB[:, :HS] = d_key.astype(BF16)
-    DKVB[:, HS:] = d_value.astype(BF16)
+    DQB[:, QW : QW + HS] = d_key.astype(BF16)
+    DQB[:, QW + HS :] = d_value.astype(BF16)
 
     @pl.loop(0, N_DP)
     def _(j):
         span = pl.ds(pl.multiple_of(j * BLK, BLK), BLK)
         yy, zz = j % RING, j // RING
-        d_normed = nt(DQB[...], WQ[yy, zz]) + nt(DKVB[...], WKV[yy, zz])
+        d_normed = nt(DQB[...], W[yy, zz])
         sums = jnp.sum(d_normed * N[:, span].astype(F32), 0, keepdims=True)
         SG[j, :, :BLK] = sums / GA[0, :, span]
 
@@ -664,9 +684,9 @@
     slots = lambda n: V((N_DP, 1, n), F32)
     scratch = [
         V((SEQ, D), BF16), V((2, 1, D), F32), row(D), V((ROWS, D), BF16),
-        V((RING, RING, BLK, QW), BF16), V((RING, RING, BLK, 2 * HS), BF16), V((QW, D), BF16),
+        V((RING, RING, BLK, QW + 2 * HS), BF16), V((QW, D), BF16),
         V((BLK, HEADS * HS), BF16), V((HS, D), BF16), V((RING, RING, BLK, 2 * RING * HS), BF16),
-        V((ROWS, QW), F32), V((ROWS, 2 * HS), F32), V((ROWS, QW), BF16), V((ROWS, 2 * HS), BF16),
+        V((ROWS, QW + 2 * HS), F32), V((ROWS, QW + 2 * HS), BF16),
         V((GROUP, ROWS, ROWS), F32), V((ROWS, QW), BF16), V((QW, ROWS), BF16), V((QW, ROWS), BF16),
         V((ROWS, D), BF16), V((2, 32, D), BF16), V((2, SEQ, D), BF16),
         V((SEQ, D), BF16), V((SEQ, D), BF16), V((SEQ, 2 * RING * HS), F32),
@@ -676,8 +696,8 @@
         row(D), slots(D), V((N_DP, D), F32), slots(HS), slots(HS), V((HEADS, HS), F32),
         row(HEADS * HS + HS), slots(HEADS * HS + HS), V((N_DP, HEADS * HS), F32), slots(BLK), slots(BLK),
         row(D), V((2, N_DP, HS), F32), V((2, N_DP, D), F32), V((SEQ, D), F32), V((SEQ, 2 * RING * HS), BF16),
-        V((ROWS, D), BF16), V((ROWS, HALF), BF16), V((ROWS, QW), F32), V((ROWS, QW), BF16),
-        V((ROWS, 2 * HS), BF16), V((QW, HALF), BF16), V((2, 64, HALF), BF16), V((5, HS, HALF), BF16),
+        V((ROWS, D), BF16), V((ROWS, HALF), BF16), V((ROWS, QW), F32), V((ROWS, QW + 2 * HS), BF16),
+        V((QW, HALF), BF16), V((2, 64, HALF), BF16), V((5, HS, HALF), BF16),
         slots(2 * BLK), slots(2 * BLK), row(2 * BLK), row(2 * BLK),
         pltpu.SemaphoreType.DMA((N_SEMS,)), pltpu.SemaphoreType.DMA((N_SEMS,)), pltpu.SemaphoreType.DMA((8,)),
     ]

time: 200 us -> 195 us (0.975)
  Pallas kernels: 193 us -> 189 us
    pallas_call x1, Pallas kernels: 193 us -> 189 us  [body(): pl.pallas_call(kernel, out_shape=(jax.ShapeDtypeStruct((1, 2), F32), jax....]
where the time goes in v2:
time: 195 us
  Pallas kernels  189 us (97%)
  local copies, waits for them, and re-layouts  4.76 us (2%)
    pallas_call x1, Pallas kernels, body(): pl.pallas_call(kernel, out_shape=(jax.ShapeDtypeStruct((1, 2), F32), jax....  189 us
    unnamed x5, local copies, waits for them, and re-layouts  4.76 us

profile of v2, /device:TPU:1, one launch (start us, length us, event | category | flops | bytes accessed | tf_op | source)
XLA Modules:
  0.0 195.1 jit_solution(5058995502326755847)
XLA Ops:
  1.3 189.0 %shard_map.103 = (f32[1,2]{1,0:T(1,128)}, f32[1,1,128,4096]{3,2,1,0:T(8,128)}, f32[1,1,256]{2,1,0:T(1,128)}) custom-call(bf16[1,1,2,64,4096]{4,3,2,1,0:T(8,128)(2,1)} %emb.1, s32[1,2]{1,0:T(1,128)} %lens.1, s32[1]{0:T(128)S(6)} %copy.14.route, bf16[1,1,256,2048]{3,2,1,0:T(8,128)(2,1)} %wq.1, bf16[1,1,256,1024]{3,2,1,0:T(8,128)(2,1)} %wkv.1, ...), custom_call_target="tpu_custom_call" | custom-call | tf_op jit(solution)/shard_map/pallas_call | solution.py:704
  190.3 1.1 copy.15
  191.4 0.0 copy-start
  191.4 3.1 %copy.16 = f32[1,1,128,4096]{3,2,1,0:T(8,128)} copy(f32[1,1,128,4096]{3,2,1,0:T(8,128)} %get-tuple-element.7) | data formatting | bytes 4194304
  194.5 0.0 copy-done
  194.5 0.6 copy.17
Async XLA Ops:
  191.4 3.1 %copy-start = (f32[1,1,256]{2,1,0:T(1,128)S(1)}, f32[1,1,256]{2,1,0:T(1,128)}, u32[]{:S(2)}) copy-start(f32[1,1,256]{2,1,0:T(1,128)} %get-tuple-element.8) | copy-start | bytes 3076

commit v3 on v2

--- a/solution.py
+++ b/solution.py
@@ -20,6 +20,7 @@
 ROWS = RING * SEQ
 BLK = D // N_DP
 HALF = D // 2
+QUART = D // 4
 SCALE = HS ** (-0.5)
 N_SEMS = 160
 
@@ -315,8 +316,6 @@
          ("wo_cr", wo_rows(yr), wo_rows(yr), {"section": 1}))
     recv(is1, ("azR", a_half(zo, 0)), ("azL", a_half(zo, 1)))
     a_item = lambda yy: WKV1.at[yy, :, LO]
-    send(is1, ("ayr", a_item(y), a_item(y), {"dp": at_yr}), ("ayl", a_item(y), a_item(y), {"dp": at_yl}),
-         ("ac", a_item(y), a_item(y), {"section": 0}))
 
     r_i = lax.broadcasted_iota(jnp.int32, (ROWS, ROWS), 0)
     c_i = lax.broadcasted_iota(jnp.int32, (ROWS, ROWS), 1)
@@ -336,6 +335,8 @@
     recv(is0, ("wo_R", wo_half(yo, 0)), ("wo_L", wo_half(yo, 1)))
     send(is0, ("wo_co", wo_rows(yo), wo_rows(yo), {"section": 1}))
     recv(is1, ("wo_c", wo_rows(y)), ("wo_cl", wo_rows(yl)), ("wo_cr", wo_rows(yr)), ("wo_co", wo_rows(yo)))
+    send(is1, ("ayr", a_item(y), a_item(y), {"dp": at_yr}), ("ayl", a_item(y), a_item(y), {"dp": at_yl}),
+         ("ac", a_item(y), a_item(y), {"section": 0}))
 
     @pl.loop(0, 8)
     def _(t):
@@ -552,17 +553,22 @@
         NL[...] += jnp.sum(d_normed * unit, 0, keepdims=True)
         pulled = d_normed * GA[1]
         d_rows = scale * (pulled - unit * jnp.mean(pulled * unit, -1, keepdims=True))
-        G[pl.ds(pl.multiple_of(z * SEQ + g * 16, 16), 16), :] = (
-            d_rows + jnp.where(last, HL[...], 0.0)
-        ).astype(BF16)
-
-    ring_z1("g", G)
-    across = pl.ds(pl.multiple_of(other * HALF, HALF), HALF)
-
-    def to_core(tag, zz):
-        send(None, (tag, G.at[my_rows(zz), across], GP.at[my_rows(zz)], {"section": other}))
-
-    to_core("gp0", z)
+        d_rows = (d_rows + jnp.where(last, HL[...], 0.0)).astype(BF16)
+        own = pl.ds(pl.multiple_of(z * SEQ + g * 16, 16), 16)
+        for c in range(2):
+            for half in range(2):
+                first = half * HALF + c * QUART
+                G[c, own, half * QUART : (half + 1) * QUART] = d_rows[:, first : first + QUART]
+
+    across = pl.ds(pl.multiple_of(other * QUART, QUART), QUART)
+
+    def to_core(c, n, zz):
+        send(None, (f"gp{c}{n}", G.at[c, my_rows(zz), across], GP.at[c, my_rows(zz)], {"section": other}))
+
+    for c in range(2):
+        ring_z1(f"g{c}", G.at[c])
+    for c in range(2):
+        to_core(c, 0, z)
 
     recv(is1, ("xc", XC.at[0]), ("gc", GC.at[0]))
 
@@ -573,51 +579,63 @@
         @pl.loop(0, 8)
         def _(t):
             span = pl.ds(pl.multiple_of(t * 512, 512), 512)
-            grad_out[0, 0, :, span] = tn(rows_a, GC[0, :, span].astype(BF16)) + tn(
-                rows_b, GC[1, :, span].astype(BF16)
-            )
+            grad_out[0, 0, :, span] = (
+                tn(rows_a, GC[0, :, span].astype(BF16)) + tn(rows_b, GC[1, :, span].astype(BF16))
+            ).astype(BF16)
 
     for h in range(N_DP):
         SG[h, :, BLK:] = NL[:, h * BLK : (h + 1) * BLK]
 
-    ring_z2("g", G)
-    to_core("gp1", zl)
-    to_core("gp2", zr)
-    ring_z3("g", G)
-    to_core("gp3", zo)
-
-    recv(None, ("ctt", CTP), ("gp0", GP.at[my_rows(z)]), ("gp1", GP.at[my_rows(zl)]),
-         ("gp2", GP.at[my_rows(zr)]), ("gp3", GP.at[my_rows(zo)]))
-
-    @pl.loop(0, 4)
-    def _(t):
-        span = pl.ds(pl.multiple_of(t * 512, 512), 512)
-        here = pl.ds(pl.multiple_of(s * HALF + t * 512, 512), 512)
-        GOP[:, span] = (mm(CTT[...], G[:, here]) + mm(CTP[...], GP[:, span])).astype(BF16)
-
-    def head_rows(yy):
-        return GOP.at[pl.ds(pl.multiple_of(yy * HS, HS), HS)]
-
-    def head_half(yy, half):
-        return GOP.at[pl.ds(pl.multiple_of(yy * HS + half * 64, 64), 64)]
-
-    send(None, ("r1r", head_half(yo, 0), FWD2.at[0], {"dp": at_yr}),
-         ("r1l", head_half(yo, 1), FWD2.at[1], {"dp": at_yl}))
-    send(is1, ("rc", head_rows(y), LAND2.at[4], {"section": 0}))
+    for c in range(2):
+        ring_z2(f"g{c}", G.at[c])
+        to_core(c, 1, zl)
+        to_core(c, 2, zr)
+
+    recv(None, ("ctt", CTP))
+
+    def head_rows(c, yy):
+        return GOP.at[c, pl.ds(pl.multiple_of(yy * HS, HS), HS)]
+
+    def head_half(c, yy, half):
+        return GOP.at[c, pl.ds(pl.multiple_of(yy * HS + half * 64, 64), 64)]
+
+    def scatter1(c):
+        ring_z3(f"g{c}", G.at[c])
+        to_core(c, 3, zo)
+        recv(None, *[(f"gp{c}{n}", GP.at[c, my_rows(zz)]) for n, zz in enumerate((z, zl, zr, zo))])
+
+        @pl.loop(0, 2)
+        def _(u):
+            span = pl.ds(pl.multiple_of(u * 512, 512), 512)
+            here = pl.ds(pl.multiple_of(s * QUART + u * 512, 512), 512)
+            GOP[c, :, span] = (mm(CTT[...], G[c, :, here]) + mm(CTP[...], GP[c, :, span])).astype(BF16)
+
+        send(None, (f"r1r{c}", head_half(c, yo, 0), FWD2.at[c, 0], {"dp": at_yr}),
+             (f"r1l{c}", head_half(c, yo, 1), FWD2.at[c, 1], {"dp": at_yl}))
+        send(is1, (f"rc{c}", head_rows(c, y), LAND2.at[c, 4], {"section": 0}))
+
+    def scatter2(c):
+        for side, tag, dest, at in ((0, "r1r", yr, at_yr), (1, "r1l", yl, at_yl)):
+            recv(None, (f"{tag}{c}", FWD2.at[c, side]))
+            rows = pl.ds(pl.multiple_of(dest * HS + side * 64, 64), 64)
+            GOP[c, rows, :] = (GOP[c, rows, :].astype(F32) + FWD2[c, side].astype(F32)).astype(BF16)
+            send(is0, (f"ra{side}{c}", head_rows(c, dest), LAND2.at[c, side], {"dp": at, "section": 0}))
+            send(is1, (f"rb{side}{c}", head_rows(c, dest), LAND2.at[c, 2 + side], {"dp": at, "section": 0}))
+
+    scatter1(0)
+    scatter1(1)
+    scatter2(0)
 
     DCT[...] = jnp.zeros_like(DCT)
 
     @pl.loop(0, 8)
     def _(t):
-        span = pl.ds(pl.multiple_of(t * 512, 512), 512)
-        DCT[...] += nt(G[:, span], WO[:, span])
-
-    for side, tag, dest, at in ((0, "r1r", yr, at_yr), (1, "r1l", yl, at_yl)):
-        recv(None, (tag, FWD2.at[side]))
-        rows = pl.ds(pl.multiple_of(dest * HS + side * 64, 64), 64)
-        GOP[rows, :] = (GOP[rows, :].astype(F32) + FWD2[side].astype(F32)).astype(BF16)
-        send(is0, (f"ra{side}", head_rows(dest), LAND2.at[side], {"dp": at, "section": 0}))
-        send(is1, (f"rb{side}", head_rows(dest), LAND2.at[2 + side], {"dp": at, "section": 0}))
+        c, u = t // RING, t % RING
+        span = pl.ds(pl.multiple_of(u * 512, 512), 512)
+        here = pl.ds(pl.multiple_of((u // 2) * HALF + c * QUART + (u % 2) * 512, 512), 512)
+        DCT[...] += nt(G[c, :, span], WO[:, here])
+
+    scatter2(1)
 
     d_key = jnp.zeros((ROWS, HS), F32)
     d_value = jnp.zeros((ROWS, HS), F32)
@@ -651,11 +669,14 @@
     SP[...] = total
     send(None, ("sp", SP, PG, {"section": other}))
 
-    recv(is0, ("rc", LAND2.at[4]), ("ra0", LAND2.at[0]), ("ra1", LAND2.at[1]),
-         ("rb0", LAND2.at[2]), ("rb1", LAND2.at[3]))
     recv(None, ("sp", PG))
     both = total + PG[...]
     gain_out[0] = jnp.where(is0, both[:, :BLK], both[:, BLK:])
+
+    for c in range(2):
+        recv(is0, (f"rc{c}", LAND2.at[c, 4]), *[
+            (f"r{kind}{side}{c}", LAND2.at[c, 2 * n + side]) for n, kind in enumerate("ab") for side in range(2)
+        ])
 
     @pl.when(is0)
     def _():
@@ -663,12 +684,13 @@
         def _(g):
             part = pl.ds(pl.multiple_of(g * 16, 16), 16)
             own = pl.ds(pl.multiple_of(y * HS + g * 16, 16), 16)
-            grad_out[0, 0, part, pl.ds(0, HALF)] = GOP[own, :].astype(F32) + (
-                LAND2[0, part, :].astype(F32) + LAND2[1, part, :].astype(F32)
-            )
-            grad_out[0, 0, part, pl.ds(HALF, HALF)] = LAND2[4, part, :].astype(F32) + (
-                LAND2[2, part, :].astype(F32) + LAND2[3, part, :].astype(F32)
-            )
+            for c in range(2):
+                grad_out[0, 0, part, c * QUART : (c + 1) * QUART] = (GOP[c, own, :].astype(F32) + (
+                    LAND2[c, 0, part, :].astype(F32) + LAND2[c, 1, part, :].astype(F32)
+                )).astype(BF16)
+                grad_out[0, 0, part, HALF + c * QUART : HALF + (c + 1) * QUART] = (LAND2[c, 4, part, :].astype(F32) + (
+                    LAND2[c, 2, part, :].astype(F32) + LAND2[c, 3, part, :].astype(F32)
+                )).astype(BF16)
 
     for cond, fin in pending:
         guarded(cond, fin)
@@ -696,16 +718,16 @@
         row(D), slots(D), V((N_DP, D), F32), slots(HS), slots(HS), V((HEADS, HS), F32),
         row(HEADS * HS + HS), slots(HEADS * HS + HS), V((N_DP, HEADS * HS), F32), slots(BLK), slots(BLK),
         row(D), V((2, N_DP, HS), F32), V((2, N_DP, D), F32), V((SEQ, D), F32), V((SEQ, 2 * RING * HS), BF16),
-        V((ROWS, D), BF16), V((ROWS, HALF), BF16), V((ROWS, QW), F32), V((ROWS, QW + 2 * HS), BF16),
-        V((QW, HALF), BF16), V((2, 64, HALF), BF16), V((5, HS, HALF), BF16),
+        V((2, ROWS, HALF), BF16), V((2, ROWS, QUART), BF16), V((ROWS, QW), F32), V((ROWS, QW + 2 * HS), BF16),
+        V((2, QW, QUART), BF16), V((2, 2, 64, QUART), BF16), V((2, 5, HS, QUART), BF16),
         slots(2 * BLK), slots(2 * BLK), row(2 * BLK), row(2 * BLK),
         pltpu.SemaphoreType.DMA((N_SEMS,)), pltpu.SemaphoreType.DMA((N_SEMS,)), pltpu.SemaphoreType.DMA((8,)),
     ]
-    return pl.pallas_call(
+    scores, grad, gains = pl.pallas_call(
         kernel,
         out_shape=(
             jax.ShapeDtypeStruct((1, 2), F32),
-            jax.ShapeDtypeStruct((1, 1, HS, D), F32),
+            jax.ShapeDtypeStruct((1, 1, HS, D), BF16),
             jax.ShapeDtypeStruct((1, 1, BLK), F32),
         ),
         in_specs=[hbm, smem, smem, hbm, hbm, hbm, hbm, hbm],
@@ -715,6 +737,7 @@
             collective_id=0, has_side_effects=True, vmem_limit_bytes=60 * 1024 * 1024
         ),
     )(embeds, lengths, route, w_query, w_keyval, w_out, norm_gain, head)
+    return scores, grad.astype(F32), gains
 
 
 def solution(mesh):

time: 195 us -> 180 us (0.923)
  Pallas kernels: 189 us -> 175 us
  local copies, waits for them, and re-layouts: 4.76 us -> 1.08 us
  other arithmetic: 0 us -> 2.76 us
    pallas_call x1, Pallas kernels: 189 us -> 175 us  [body(): pl.pallas_call(kernel, out_shape=(jax.ShapeDtypeStruct((1, 2), F32), jax....]
    unnamed x5 -> x6, local copies, waits for them, and re-layouts: 4.76 us -> 1.08 us
    convert_element_type x0 -> x1, other arithmetic: none -> 2.76 us  [body(): return (scores, grad.astype(F32), gains)]
where the time goes in v3:
time: 180 us
  Pallas kernels  175 us (97%)
  other arithmetic  2.76 us (2%)
    pallas_call x1, Pallas kernels, body(): pl.pallas_call(kernel, out_shape=(jax.ShapeDtypeStruct((1, 2), F32), jax....  175 us

profile of v3, /device:TPU:1, one launch (start us, length us, event | category | flops | bytes accessed | tf_op | source)
XLA Modules:
  0.0 180.3 jit_solution(1861549843193775250)
XLA Ops:
  1.3 175.1 %shard_map.103 = (f32[1,2]{1,0:T(1,128)}, bf16[1,1,128,4096]{3,2,1,0:T(8,128)(2,1)}, f32[1,1,256]{2,1,0:T(1,128)}) custom-call(bf16[1,1,2,64,4096]{4,3,2,1,0:T(8,128)(2,1)} %emb.1, s32[1,2]{1,0:T(1,128)} %lens.1, s32[1]{0:T(128)S(6)} %copy.13.route, bf16[1,1,256,2048]{3,2,1,0:T(8,128)(2,1)} %wq.1, bf16[1,1,256,1024]{3,2,1,0:T(8,128)(2,1)} %wkv.1, ...), custom_call_target="tpu_custom_call" | custom-call | tf_op jit(solution)/shard_map/pallas_call | solution.py:726
  176.4 0.0 copy-start.1
  176.4 0.0 copy-start
  176.4 2.8 %convert_element_type.3 = f32[1,1,128,4096]{3,2,1,0:T(8,128)} convert(bf16[1,1,128,4096]{3,2,1,0:T(8,128)(2,1)} %get-tuple-element.7) | non-fusion elementwise | flops 524288 | bytes 3145728 | tf_op jit(solution)/shard_map/convert_element_type | solution.py:740
  179.2 0.0 copy-done.1
  179.2 0.5 copy.14
  179.7 0.0 copy-done
  179.7 0.6 copy.15
Async XLA Ops:
  176.4 2.8 %copy-start.1 = (f32[1,2]{1,0:T(1,128)S(1)}, f32[1,2]{1,0:T(1,128)}, u32[]{:S(2)}) copy-start(f32[1,2]{1,0:T(1,128)} %get-tuple-element.12) | copy-start | bytes 28
  176.4 3.3 %copy-start = (f32[1,1,256]{2,1,0:T(1,128)S(1)}, f32[1,1,256]{2,1,0:T(1,128)}, u32[]{:S(2)}) copy-start(f32[1,1,256]{2,1,0:T(1,128)} %get-tuple-element.14) | copy-start | bytes 3076

commit v4 on v3

--- a/solution.py
+++ b/solution.py
@@ -245,14 +245,6 @@
     send(is1, ("byR", b_half(yl, 0), b_half(yl, 0), {"dp": at_yr}))
     recv(is1, ("byl", WKV1.at[yr, z, HI]))
     send(is1, ("byL", b_half(yr, 1), b_half(yr, 1), {"dp": at_yl}))
-    ring_z2("n", N)
-    a_own = WKV1.at[y, z, LO]
-    send(is1, ("azr", a_own, a_own, {"dp": at_zr}), ("azl", a_own, a_own, {"dp": at_zl}))
-    recv(is1, ("byR", b_half(yo, 0)), ("byL", b_half(yo, 1)))
-    b_item = lambda zz: WKV1.at[:, zz, HI]
-    send(is1, ("bzr", b_item(z), b_item(z), {"dp": at_zr}), ("bzl", b_item(z), b_item(z), {"dp": at_zl}),
-         ("bc", b_item(z), b_item(z), {"section": 0}))
-
     for side, yy, fwd, at, kept in (("r", yl, "R", at_yr, (0, 2)), ("l", yr, "L", at_yl, (1, 3))):
         for n in range(RING):
             chunk = W.at[yy, order[n]]
@@ -265,6 +257,14 @@
          ("wo_r", mine, mine, {"dp": at_yr}),
          ("wo_l", mine, mine, {"dp": at_yl}),
          ("wo_c", mine, mine, {"section": 1}))
+
+    ring_z2("n", N)
+    a_own = WKV1.at[y, z, LO]
+    send(is1, ("azr", a_own, a_own, {"dp": at_zr}), ("azl", a_own, a_own, {"dp": at_zl}))
+    recv(is1, ("byR", b_half(yo, 0)), ("byL", b_half(yo, 1)))
+    b_item = lambda zz: WKV1.at[:, zz, HI]
+    send(is1, ("bzr", b_item(z), b_item(z), {"dp": at_zr}), ("bzl", b_item(z), b_item(z), {"dp": at_zl}),
+         ("bc", b_item(z), b_item(z), {"section": 0}))
 
     a_half = lambda zz, half: WKV1.at[y, zz, pl.ds(64 * half, 64)]
     recv(is1, ("azr", WKV1.at[y, zl, LO]))
@@ -338,23 +338,29 @@
     send(is1, ("ayr", a_item(y), a_item(y), {"dp": at_yr}), ("ayl", a_item(y), a_item(y), {"dp": at_yl}),
          ("ac", a_item(y), a_item(y), {"section": 0}))
 
-    @pl.loop(0, 8)
-    def _(t):
-        span = pl.ds(pl.multiple_of(t * 512, 512), 512)
-        OP[:, span] = mm(CTX[...], WO[:, span]).astype(BF16)
-
-    send(None, ("o1r", half_rows(OP, zo, 0), FWD.at[0], {"dp": at_zr}),
-         ("o1l", half_rows(OP, zo, 1), FWD.at[1], {"dp": at_zl}))
-    for side, tag, dest, at in ((0, "o1r", zr, at_zr), (1, "o1l", zl, at_zl)):
-        recv(None, (tag, FWD.at[side]))
-
-        @pl.loop(0, 2)
-        def _(g):
-            rows = pl.ds(pl.multiple_of(dest * SEQ + side * 32 + g * 16, 16), 16)
-            part = pl.ds(pl.multiple_of(g * 16, 16), 16)
-            OP[rows, :] = (OP[rows, :].astype(F32) + FWD[side, part, :].astype(F32)).astype(BF16)
-
-        send(None, (f"o2{side}", OP.at[my_rows(dest)], LAND.at[side], {"dp": at}))
+    for c in range(2):
+        @pl.loop(RING * c, RING * (c + 1))
+        def _(t):
+            span = pl.ds(pl.multiple_of(t * 512, 512), 512)
+            OP[:, span] = mm(CTX[...], WO[:, span]).astype(BF16)
+
+        side_cols = pl.ds(c * HALF, HALF)
+        send(None, (f"o1r{c}", half_rows(OP, zo, 0).at[:, side_cols], FWD.at[0, :, side_cols], {"dp": at_zr}),
+             (f"o1l{c}", half_rows(OP, zo, 1).at[:, side_cols], FWD.at[1, :, side_cols], {"dp": at_zl}))
+    for c in range(2):
+        side_cols = pl.ds(c * HALF, HALF)
+        for side, tag, dest, at in ((0, "o1r", zr, at_zr), (1, "o1l", zl, at_zl)):
+            recv(None, (f"{tag}{c}", FWD.at[side, :, side_cols]))
+
+            @pl.loop(0, 2)
+            def _(g):
+                rows = pl.ds(pl.multiple_of(dest * SEQ + side * 32 + g * 16, 16), 16)
+                part = pl.ds(pl.multiple_of(g * 16, 16), 16)
+                OP[rows, side_cols] = (
+                    OP[rows, side_cols].astype(F32) + FWD[side, part, side_cols].astype(F32)
+                ).astype(BF16)
+
+            send(None, (f"o2{side}{c}", OP.at[my_rows(dest), side_cols], LAND.at[side, :, side_cols], {"dp": at}))
 
     a_two = lambda yy, half: WKV1.at[yy, pl.ds(2 * half, 2), LO]
     recv(is1, ("bzR", b_two(zo, 0)), ("bzL", b_two(zo, 1)))
@@ -364,7 +370,7 @@
         send(is1, ("ay" + fwd, a_two(yy, half), a_two(yy, half), {"dp": at}),
              ("ac" + tag, a_item(yy), a_item(yy), {"section": 0}))
 
-    recv(None, ("o20", LAND.at[0]), ("o21", LAND.at[1]))
+    recv(None, *[(f"o2{side}{c}", LAND.at[side, :, pl.ds(c * HALF, HALF)]) for c in range(2) for side in range(2)])
 
     length = jnp.where(is0, lens[0, 0], lens[0, 1])
     NL[...] = jnp.zeros_like(NL)

time: 180 us -> 178 us (0.989)
  Pallas kernels: 175 us -> 173 us
    pallas_call x1, Pallas kernels: 175 us -> 173 us  [body(): pl.pallas_call(kernel, out_shape=(jax.ShapeDtypeStruct((1, 2), F32), jax....]
where the time goes in v4:
time: 178 us
  Pallas kernels  173 us (97%)
  other arithmetic  2.76 us (2%)
    pallas_call x1, Pallas kernels, body(): pl.pallas_call(kernel, out_shape=(jax.ShapeDtypeStruct((1, 2), F32), jax....  173 us

profile of v4, /device:TPU:1, one launch (start us, length us, event | category | flops | bytes accessed | tf_op | source)
XLA Modules:
  0.0 177.8 jit_solution(1685508029201092006)
XLA Ops:
  1.3 172.7 %shard_map.103 = (f32[1,2]{1,0:T(1,128)}, bf16[1,1,128,4096]{3,2,1,0:T(8,128)(2,1)}, f32[1,1,256]{2,1,0:T(1,128)}) custom-call(bf16[1,1,2,64,4096]{4,3,2,1,0:T(8,128)(2,1)} %emb.1, s32[1,2]{1,0:T(1,128)} %lens.1, s32[1]{0:T(128)S(6)} %copy.13.route, bf16[1,1,256,2048]{3,2,1,0:T(8,128)(2,1)} %wq.1, bf16[1,1,256,1024]{3,2,1,0:T(8,128)(2,1)} %wkv.1, ...), custom_call_target="tpu_custom_call" | custom-call | tf_op jit(solution)/shard_map/pallas_call | solution.py:732
  173.9 0.0 copy-start.1
  174.0 0.0 copy-start
  174.0 2.8 %convert_element_type.3 = f32[1,1,128,4096]{3,2,1,0:T(8,128)} convert(bf16[1,1,128,4096]{3,2,1,0:T(8,128)(2,1)} %get-tuple-element.7) | non-fusion elementwise | flops 524288 | bytes 3145728 | tf_op jit(solution)/shard_map/convert_element_type | solution.py:746
  176.7 0.0 copy-done.1
  176.7 0.5 copy.14
  177.2 0.0 copy-done
  177.2 0.6 copy.15
Async XLA Ops:
  173.9 2.8 %copy-start.1 = (f32[1,2]{1,0:T(1,128)S(1)}, f32[1,2]{1,0:T(1,128)}, u32[]{:S(2)}) copy-start(f32[1,2]{1,0:T(1,128)} %get-tuple-element.12) | copy-start | bytes 28
  174.0 3.3 %copy-start = (f32[1,1,256]{2,1,0:T(1,128)S(1)}, f32[1,1,256]{2,1,0:T(1,128)}, u32[]{:S(2)}) copy-start(f32[1,1,256]{2,1,0:T(1,128)} %get-tuple-element.14) | copy-start | bytes 3076
